TPU v7x, 768 devices: a whole 4x8x12 slice. The times are simulated.
768 devices in a mesh: lat: 96 (over x, z, core), lon: 8 (over y).
Axes of the slice: x: 4, y: 8, z: 12, core: 2. Of those that a mesh axis runs over, the one named last changes fastest.
Arguments:
- nodes: bfloat16 [196608, 256], P(('lat', 'lon')), may hold values from -6 to 6
- edges: bfloat16 [2359296, 256], P(('lat', 'lon')), may hold values from -6 to 6
- senders: int32 [2359296], P(('lat', 'lon')), may hold values from 0 to 1023, as said below
- receivers: int32 [2359296], P(('lat', 'lon')), may hold values from 0 to 255
- edge_count: int32 [768], P(('lat', 'lon')), may hold values from 1536 to 3072, as said below
- send_index: int32 [6144, 64], P(('lat', 'lon')), may hold values from 0 to 255
- rim_index: int32 [1536, 128], P(('lat', 'lon')), may hold values from 0 to 255
- edge_w1: bfloat16 [768, 256], replicated, may hold values from -0.21875 to 0.21875
- edge_b1: float32 [256], replicated, may hold values from -3 to 3
- edge_w2: bfloat16 [256, 256], replicated, may hold values from -0.375 to 0.375
- edge_gain: float32 [256], replicated, may hold values from 0.1 to 1.9
- node_w1: bfloat16 [512, 256], replicated, may hold values from -0.25 to 0.25
- node_b1: float32 [256], replicated, may hold values from -3 to 3
- node_w2: bfloat16 [256, 256], replicated, may hold values from -0.375 to 0.375
- node_gain: float32 [256], replicated, may hold values from 0.1 to 1.9
Outputs:
- new_nodes: bfloat16 [196608, 256], P(('lat', 'lon'))
- new_edges: bfloat16 [2359296, 256], P(('lat', 'lon'))
Inputs may be any that keep to these rules, and one draw needn't show every extreme that they name: `senders`: A sender in the first band never names the slots of the band before it, one in the last band never those of the band after it. `edge_count`: some device has all 3072 slots live.
All inputs are finite; a program needn't handle non-finite values.
Results may differ from a plain program's by a relative error of at most 0.009.
Values may be sent and summed in bfloat16 or wider, within the bound.
No kernel may reach another device: no remote copies, remote signals or barrier semaphores. Data moves between devices by JAX's collectives and lax.ppermute only.
A program may use at most 32 MiB of HBM per device.

v0:
```python
import jax
import jax.numpy as jnp
from jax import lax
from jax.sharding import PartitionSpec as P


def passed_along(block, axis, distance):
    devices = range(lax.axis_size(axis))
    route = [(i - distance, i) for i in devices if i - distance in devices]
    return lax.ppermute(block, axis, route)


def layer_norm(values, gain):
    mean = jnp.mean(values, axis=-1, keepdims=True)
    centred = values - mean
    var = jnp.mean(centred * centred, axis=-1, keepdims=True)
    return centred * lax.rsqrt(var + 1e-05) * gain


def local(
    nodes,
    edges,
    senders,
    receivers,
    edge_count,
    send_index,
    rim_index,
    edge_w1,
    edge_b1,
    edge_w2,
    edge_gain,
    node_w1,
    node_b1,
    node_w2,
    node_gain,
):
    n_lon = lax.axis_size("lon")
    node_rows, width = nodes.shape
    edge_rows = edges.shape[0]
    halo_rows = send_index.shape[1]
    band_nodes, band_lists = (
        lax.all_gather(nodes, "lon", axis=0, tiled=True),
        lax.all_gather(send_index, "lon", axis=0, tiled=True),
    )
    mine = lax.axis_index("lon")
    lists = jnp.take(band_lists.reshape(n_lon, n_lon, halo_rows), mine, axis=1)
    lists = lists + (jnp.arange(n_lon, dtype=jnp.int32) * node_rows)[:, None]
    incoming = band_nodes[lists.reshape(-1)]
    from_below = passed_along(nodes[rim_index[0]], "lat", 1)
    from_above = passed_along(nodes[rim_index[1]], "lat", -1)
    table = jnp.concatenate([nodes, incoming, from_below, from_above], axis=0)
    pre = jnp.dot(edges, edge_w1[:width], preferred_element_type=jnp.float32)
    pre = pre + jnp.dot(
        table[senders], edge_w1[width : 2 * width], preferred_element_type=jnp.float32
    )
    pre = pre + jnp.dot(nodes[receivers], edge_w1[2 * width :], preferred_element_type=jnp.float32)
    hidden = jax.nn.silu(pre + edge_b1).astype(jnp.bfloat16)
    update = layer_norm(jnp.dot(hidden, edge_w2, preferred_element_type=jnp.float32), edge_gain)
    live = jnp.arange(edge_rows, dtype=jnp.int32) < edge_count[0]
    update = jnp.where(live[:, None], update, 0.0).astype(jnp.bfloat16)
    new_edges = (edges.astype(jnp.float32) + update.astype(jnp.float32)).astype(jnp.bfloat16)
    member = (receivers[None, :] == jnp.arange(node_rows, dtype=jnp.int32)[:, None]).astype(
        jnp.bfloat16
    )
    messages = jnp.dot(member, update, preferred_element_type=jnp.float32).astype(jnp.bfloat16)
    node_pre = jnp.dot(nodes, node_w1[:width], preferred_element_type=jnp.float32)
    node_pre = node_pre + jnp.dot(messages, node_w1[width:], preferred_element_type=jnp.float32)
    node_hidden = jax.nn.silu(node_pre + node_b1).astype(jnp.bfloat16)
    node_out = layer_norm(
        jnp.dot(node_hidden, node_w2, preferred_element_type=jnp.float32), node_gain
    )
    new_nodes = (nodes.astype(jnp.float32) + node_out).astype(jnp.bfloat16)
    return (new_nodes, new_edges)


def solution(mesh):
    return jax.shard_map(
        local,
        mesh=mesh,
        in_specs=(
            P(("lat", "lon"), None),
            P(("lat", "lon"), None),
            P(("lat", "lon")),
            P(("lat", "lon")),
            P(("lat", "lon")),
            P(("lat", "lon"), None),
            P(("lat", "lon"), None),
            P(),
            P(),
            P(),
            P(),
            P(),
            P(),
            P(),
            P(),
        ),
        out_specs=(P(("lat", "lon"), None), P(("lat", "lon"), None)),
        check_vma=False,
    )
```

profile of v0, /device:TPU:6, one launch (start us, length us, event | category | flops | bytes accessed | tf_op | source)
XLA Modules:
  0.0 115.5 jit_solution(11715708476349331777)
XLA Ops:
  7.2 0.0 copy-start
  7.2 0.0 copy-start.1
  7.2 0.0 all-gather.2.cloned.1.call-start
  7.2 0.7 all-gather.2.cloned.1.call-update
  7.9 0.8 fusion.18
  8.7 1.7 %gather_fusion.1 = bf16[128,256]{1,0:T(8,128)(2,1)S(1)} fusion(bf16[256,256]{1,0:T(8,128)(2,1)} %param.15, s32[1024]{0:T(1024)S(1)} %pad_clamp_fusion.1), kind=kCustom, calls=%fused_computation.1 | custom fusion | bytes 131584 | tf_op jit(solution)/shard_map/gather | solution.py:49
  10.4 1.9 %collective-permute-start = (bf16[128,256]{1,0:T(8,128)(2,1)S(1)}, bf16[128,256]{1,0:T(8,128)(2,1)S(1)}, u32[]{:S(2)}, u32[]{:S(2)}) collective-permute-start(bf16[128,256]{1,0:T(8,128)(2,1)S(1)} %gather_fusion.1), channel_id=1, source_target_pairs={{0,8},{8,16},{16,24},{24,32},{32,40},{40,48},{48,56},{56,64},{64,7... | collective-permute-start | bytes 196616 | tf_op jit(solution)/shard_map/ppermute | solution.py:10
  12.3 1.7 %gather_fusion.2 = bf16[128,256]{1,0:T(8,128)(2,1)S(1)} fusion(bf16[256,256]{1,0:T(8,128)(2,1)} %param.15, s32[1024]{0:T(1024)S(1)} %pad_clamp_fusion), kind=kCustom, calls=%fused_computation.2 | custom fusion | bytes 131584 | tf_op jit(solution)/shard_map/gather | solution.py:50
  14.0 14.3 %collective-permute-start.1 = (bf16[128,256]{1,0:T(8,128)(2,1)S(1)}, bf16[128,256]{1,0:T(8,128)(2,1)S(1)}, u32[]{:S(2)}, u32[]{:S(2)}) collective-permute-start(bf16[128,256]{1,0:T(8,128)(2,1)S(1)} %gather_fusion.2), channel_id=1, source_target_pairs={{8,0},{16,8},{24,16},{32,24},{40,32},{48,40},{56,48},{64,56},{72,6... | collective-permute-start | bytes 196616 | tf_op jit(solution)/shard_map/ppermute | solution.py:10
  28.3 1.0 copy.17
  29.3 26.2 %all_gather.7 = s32[64,64]{1,0:T(8,128)S(1)} all-gather(s32[8,64]{1,0:T(8,128)} %param.20), channel_id=1, replica_groups=mesh['lat'=96,'lon'=8] {'lon'}, dimensions={0}, use_global_device_ids=true | all-gather | bytes 18432 | tf_op jit(solution)/shard_map/all_gather | solution.py:43
  55.5 0.1 broadcast_add_fusion
  55.6 0.1 add.132
  55.7 0.7 fusion.17
  56.4 13.0 %gather_fusion.4 = bf16[3072,256]{1,0:T(8,128)(2,1)} fusion(bf16[256,256]{1,0:T(8,128)(2,1)S(1)} %copy-done.1, s32[3072]{0:T(1024)S(1)} %fusion.17), kind=kCustom, calls=%fused_computation.4 | custom fusion | bytes 3158016 | tf_op jit(solution)/shard_map/gather | solution.py:56
  70.2 1.8 %copy.18 = bf16[3072,256]{0,1:T(8,128)(2,1)} copy(bf16[3072,256]{1,0:T(8,128)(2,1)S(1)} %copy-done.2) | data formatting | bytes 3145728 | tf_op args[1]
  72.0 0.9 fusion.14
  72.9 2.2 %fusion.12 = f32[3072,256]{1,0:T(8,128)} fusion(bf16[3072,256]{1,0:T(8,128)(2,1)S(1)} %copy-done.2, bf16[768,256]{1,0:T(8,128)(2,1)S(1)} %copy-done.4), kind=kOutput, calls=%fused_computation.28 | convolution fusion | flops 402653184 | bytes 4849664 | tf_op jit(solution)/shard_map/dot_general | solution.py:52
  75.1 2.9 %gather_fusion = bf16[512,256]{1,0:T(8,128)(2,1)S(1)} fusion(bf16[2048,256]{1,0:T(8,128)(2,1)} %all-gather.2.cloned.1.call-done, s32[1024]{0:T(1024)S(1)} %pad_clamp_fusion.2), kind=kCustom, calls=%fused_computation | custom fusion | bytes 526336 | tf_op jit(solution)/shard_map/gather | solution.py:48
  78.1 11.1 %gather_fusion.3 = bf16[3072,256]{1,0:T(8,128)(2,1)S(1)} fusion(bf16[1024,256]{1,0:T(8,128)(2,1)S(1)} %pad_maximum_fusion, s32[3072]{0:T(1024)S(1)} %fusion.16), kind=kCustom, calls=%fused_computation.3 | custom fusion | bytes 3158016 | tf_op jit(solution)/shard_map/gather | solution.py:54
  89.2 0.0 copy-start.10
  89.2 4.1 %convolution_add_fusion.1 = f32[3072,256]{1,0:T(8,128)} fusion(f32[3072,256]{1,0:T(8,128)} %fusion.12, bf16[3072,256]{1,0:T(8,128)(2,1)S(1)} %gather_fusion.3, bf16[768,256]{1,0:T(8,128)(2,1)S(1)} %copy-done.4), kind=kOutput, calls=%fused_computation.7 | convolution fusion | flops 403439616 | bytes 7995392 | tf_op jit(solution)/shard_map/dot_general | solution.py:53
  93.3 3.7 %fusion.21 = (f32[3072]{0:T(1024)S(1)}, f32[3072,256]{0,1:T(8,128)S(1)}) fusion(bf16[256,256]{1,0:T(8,128)(2,1)S(1)} %copy-done, f32[3072,256]{1,0:T(8,128)} %convolution_add_fusion.1, bf16[3072,256]{1,0:T(8,128)(2,1)} %gather_fusion.4, f32[256]{0:T(256)S(1)} %copy-done.10, bf16[768,256]{1,0:T(8,128)(2,1)} %param.22), kind=kOutput, calls=%fused_computation.53 | convolution fusion | flops 811594752 | bytes 8139776 | tf_op jit(solution)/shard_map/dot_general | solution.py:58
  97.0 0.3 multiply_reduce_fusion
  97.4 1.0 copy-done.3
  98.4 1.9 %add_convert_fusion = bf16[3072,256]{0,1:T(8,128)(2,1)} fusion(bf16[3072,256]{0,1:T(8,128)(2,1)S(1)} %copy-done.3, f32[256]{0:T(256)S(1)} %copy-done.9, f32[3072]{0:T(1024)S(1)} %add_rsqrt_fusion, f32[3072,256]{0,1:T(8,128)S(1)} %get-tuple-element.18, f32[3072]{0:T(1024)S(1)} %broadcast_multiply_fusion, pred[3072]{0:T(1024)(128)(4,1)S(1)} %iota_compare_fusion.8), kind=kLoop, calls=%fused_computation.8 | loop fusion | flops 7077888 | bytes 6320128 | tf_op jit(solution)/shard_map/convert_element_type | solution.py:61
  100.3 2.6 %copy.20 = bf16[3072,256]{1,0:T(8,128)(2,1)} copy(bf16[3072,256]{0,1:T(8,128)(2,1)} %add_convert_fusion) | data formatting | bytes 3145728
  102.8 3.0 %multiply_convert_fusion.1 = bf16[256,256]{1,0:T(8,128)(2,1)} fusion(f32[256,256]{1,0:T(8,128)} %fusion.14, s32[3072]{0:T(1024)} %param.18, f32[256]{0:T(256)} %param.27, bf16[512,256]{1,0:T(8,128)(2,1)} %param.26, f32[3072,256]{0,1:T(8,128)S(1)} %get-tuple-element.18, f32[256]{0:T(256)} %param.25, f32[3072]{0:T(1024)} %copy-done.7, ...), kind=kOutput, calls=%fused_computation.24 | convolution fusion | flops 441450496 | bytes 3712000 | tf_op jit(solution)/shard_map/dot_general | solution.py:67
  105.8 1.2 %fusion.24 = (f32[256]{0:T(256)S(1)}, f32[256,256]{0,1:T(8,128)S(1)}) fusion(bf16[256,256]{1,0:T(8,128)(2,1)} %multiply_convert_fusion.1, bf16[256,256]{1,0:T(8,128)(2,1)S(1)} %copy-done.5), kind=kOutput, calls=%fused_computation.54 | convolution fusion | flops 33619712 | bytes 525312 | tf_op jit(solution)/shard_map/dot_general | solution.py:70
  107.0 0.1 multiply_reduce_fusion.1
  107.1 0.8 add_convert_fusion.1
  107.9 0.8 copy.19
  (34 shorter events, 0.2 us)
Async XLA Ops:
  7.2 86.1 %copy-start = (bf16[256,256]{1,0:T(8,128)(2,1)S(1)}, bf16[256,256]{1,0:T(8,128)(2,1)}, u32[]{:S(2)}) copy-start(bf16[256,256]{1,0:T(8,128)(2,1)} %param.24) | copy-start | bytes 393220
  7.2 49.2 %copy-start.1 = (bf16[256,256]{1,0:T(8,128)(2,1)S(1)}, bf16[256,256]{1,0:T(8,128)(2,1)}, u32[]{:S(2)}) copy-start(bf16[256,256]{1,0:T(8,128)(2,1)} %param.15) | copy-start | bytes 393220
  7.2 67.9 %all-gather.2.cloned.1.call-start = ((), (), s32[]{:S(2)}) async-start(), calls=%async_computation | async-start | bytes 1179648 | tf_op jit(solution)/shard_map/all_gather | solution.py:42
  10.4 67.7 %collective-permute-start = (bf16[128,256]{1,0:T(8,128)(2,1)S(1)}, bf16[128,256]{1,0:T(8,128)(2,1)S(1)}, u32[]{:S(2)}, u32[]{:S(2)}) collective-permute-start(bf16[128,256]{1,0:T(8,128)(2,1)S(1)} %gather_fusion.1), channel_id=1, source_target_pairs={{0,8},{8,16},{16,24},{24,32},{32,40},{40,48},{48,56},{56,64},{64,7... | collective-permute-start | bytes 196616 | tf_op jit(solution)/shard_map/ppermute | solution.py:10
  14.0 64.0 %collective-permute-start.1 = (bf16[128,256]{1,0:T(8,128)(2,1)S(1)}, bf16[128,256]{1,0:T(8,128)(2,1)S(1)}, u32[]{:S(2)}, u32[]{:S(2)}) collective-permute-start(bf16[128,256]{1,0:T(8,128)(2,1)S(1)} %gather_fusion.2), channel_id=1, source_target_pairs={{8,0},{16,8},{24,16},{32,24},{40,32},{48,40},{56,48},{64,56},{72,6... | collective-permute-start | bytes 196616 | tf_op jit(solution)/shard_map/ppermute | solution.py:10
  56.4 13.8 %copy-start.2 = (bf16[3072,256]{1,0:T(8,128)(2,1)S(1)}, bf16[3072,256]{1,0:T(8,128)(2,1)}, u32[]{:S(2)}) copy-start(bf16[3072,256]{1,0:T(8,128)(2,1)} %param.16) | copy-start | bytes 4718596
  69.5 2.5 %copy-start.8 = (s32[3072]{0:T(1024)S(1)}, s32[3072]{0:T(1024)}, u32[]{:S(2)}) copy-start(s32[3072]{0:T(1024)} %param.17) | copy-start | bytes 36868
  69.5 2.5 %copy-start.6 = (bf16[512,256]{1,0:T(8,128)(2,1)S(1)}, bf16[512,256]{1,0:T(8,128)(2,1)}, u32[]{:S(2)}) copy-start(bf16[512,256]{1,0:T(8,128)(2,1)} %param.26) | copy-start | bytes 786436
  69.5 3.4 %copy-start.4 = (bf16[768,256]{1,0:T(8,128)(2,1)S(1)}, bf16[768,256]{1,0:T(8,128)(2,1)}, u32[]{:S(2)}) copy-start(bf16[768,256]{1,0:T(8,128)(2,1)} %param.22) | copy-start | bytes 1179652
  89.2 4.1 %copy-start.10 = (f32[256]{0:T(256)S(1)}, f32[256]{0:T(256)}, u32[]{:S(2)}) copy-start(f32[256]{0:T(256)} %param.23) | copy-start | bytes 3076
  97.0 1.4 %copy-start.3 = (bf16[3072,256]{0,1:T(8,128)(2,1)S(1)}, bf16[3072,256]{0,1:T(8,128)(2,1)}, u32[]{:S(2)}) copy-start(bf16[3072,256]{0,1:T(8,128)(2,1)} %copy.18) | copy-start | bytes 4718596
  97.0 1.4 %copy-start.9 = (f32[256]{0:T(256)S(1)}, f32[256]{0:T(256)}, u32[]{:S(2)}) copy-start(f32[256]{0:T(256)} %param.25) | copy-start | bytes 3076
  98.4 1.9 %copy-start.7 = (f32[3072]{0:T(1024)}, f32[3072]{0:T(1024)S(1)}, u32[]{:S(2)}) copy-start(f32[3072]{0:T(1024)S(1)} %add_rsqrt_fusion) | copy-start | bytes 36868
  102.8 3.0 %copy-start.5 = (bf16[256,256]{1,0:T(8,128)(2,1)S(1)}, bf16[256,256]{1,0:T(8,128)(2,1)}, u32[]{:S(2)}) copy-start(bf16[256,256]{1,0:T(8,128)(2,1)} %param.28) | copy-start | bytes 393220
Sparse Core Ops, SparseCore 0:
  10.4 50.2 all-gather.1
where the time goes:
time: 116 us; the launch traced here: 115 us
  local copies, waits for them, and re-layouts  37.6 us (32%)
  blocking collectives  26.2 us (23%)
  starting transfers between devices  16.2 us (14%)
  matrix products  15 us (13%)
  between operations  15 us (13%)
  other arithmetic  4.73 us (4%)
    all_gather x1, blocking collectives, local(): lax.all_gather(send_index, 'lon', axis=0, tiled=True)  26.2 us
    ppermute x2, starting transfers between devices, passed_along(): return lax.ppermute(block, axis, route)  16.2 us
    gather x1, local copies, waits for them, and re-layouts, local(): nodes[receivers]  13 us
    gather x1, local copies, waits for them, and re-layouts, local(): table[senders]  11.1 us
    unnamed x26, local copies, waits for them, and re-layouts  7.15 us
    dot_general x1, matrix products, local(): jnp.dot(table[senders], edge_w1[width:2 * width], preferred_element_type=...  4.11 us
    dot_general x1, matrix products, local(): jnp.dot(hidden, edge_w2, preferred_element_type=jnp.float32)  3.67 us
    dot_general x1, matrix products, local(): jnp.dot(messages, node_w1[width:], preferred_element_type=jnp.float32)  2.99 us
  transfers between devices with their start and end apart: 3, of which 0 were waited for; matrix products, arithmetic and copies ran while one was open for 23% of the time, Pallas kernels for 0%

commit v1 on v0

v1 whole, which is shorter than its diff:
```python
import functools

import jax
import jax.numpy as jnp
from jax import lax
from jax.experimental import pallas as pl
from jax.experimental.pallas import tpu as pltpu
from jax.sharding import PartitionSpec as P

F32 = jnp.float32
BF16 = jnp.bfloat16
LANES = 128
TILE = 512


def contract(a, b, dims):
    return lax.dot_general(a, b, (dims, ((), ())), preferred_element_type=F32)


def pick_kernel(nodes_ref, send_ref, rim_ref, halo_ref, up_ref, down_ref):
    nodes = nodes_ref[...]
    rows = nodes.shape[0]
    n_lon, halo = send_ref.shape

    def picked(row):
        spots = lax.broadcasted_iota(jnp.int32, (rows, row.shape[1]), 0)
        chosen = jnp.where(spots == row, 1.0, 0.0).astype(BF16)
        return contract(chosen, nodes, ((0,), (0,))).astype(BF16)

    up_ref[...] = picked(rim_ref[0:1, :])
    down_ref[...] = picked(rim_ref[1:2, :])
    for p in range(0, n_lon, 2):
        pair = jnp.concatenate([send_ref[p : p + 1, :], send_ref[p + 1 : p + 2, :]], axis=1)
        value = picked(pair)
        halo_ref[p * halo : (p + 2) * halo, :] = value


def silu(x):
    half = 0.5 * x
    return half + half * jnp.tanh(half)


def normed(values, gain):
    mean = jnp.mean(values, axis=-1, keepdims=True)
    centred = values - mean
    var = jnp.mean(centred * centred, axis=-1, keepdims=True)
    return centred * lax.rsqrt(var + 1e-05) * gain


def main_kernel(
    count_ref,
    nodes_ref,
    halo_ref,
    below_ref,
    above_ref,
    send_col_ref,
    recv_col_ref,
    recv_row_ref,
    w1_ref,
    b1_ref,
    w2_ref,
    gain_ref,
    v1_ref,
    c1_ref,
    v2_ref,
    node_gain_ref,
    edges_hbm,
    new_nodes_ref,
    new_edges_hbm,
    edges_buf,
    out_buf,
    sender_table,
    receiver_table,
    messages,
    in_sem,
    out_sem,
):
    edge_rows, width = edges_buf.shape
    tiles = edge_rows // TILE
    node_rows = nodes_ref.shape[0]

    def load(t):
        rows = pl.ds(t * TILE, TILE)
        return pltpu.make_async_copy(edges_hbm.at[rows], edges_buf.at[rows], in_sem.at[t])

    def store(t):
        rows = pl.ds(t * TILE, TILE)
        return pltpu.make_async_copy(out_buf.at[rows], new_edges_hbm.at[rows], out_sem.at[t])

    for t in range(tiles):
        load(t).start()
    count = count_ref[0]
    nodes = nodes_ref[...]
    w_s = w1_ref[width : 2 * width, :]
    halo_rows = halo_ref.shape[0]
    rim_rows = below_ref.shape[0]

    def project(rows, start):
        sender_table[start : start + rows.shape[0], :] = contract(
            rows, w_s, ((1,), (0,))
        ).astype(BF16)

    project(nodes, 0)
    project(halo_ref[...], node_rows)
    project(below_ref[...], node_rows + halo_rows)
    project(above_ref[...], node_rows + halo_rows + rim_rows)
    receiver_table[...] = contract(nodes, w1_ref[2 * width :, :], ((1,), (0,))).astype(BF16)
    messages[...] = jnp.zeros_like(messages)
    table_rows = sender_table.shape[0]

    for t in range(tiles):
        load(t).wait()
        rows = slice(t * TILE, (t + 1) * TILE)

        @pl.when(count > t * TILE)
        def _():
            edges = edges_buf[rows, :]
            lane = lax.broadcasted_iota(jnp.int32, (TILE, LANES), 1)

            def one_hot(column, size):
                wide = jnp.broadcast_to(column, (TILE, LANES))
                return jnp.concatenate(
                    [
                        jnp.where(wide == lane + j * LANES, 1.0, 0.0).astype(BF16)
                        for j in range(size // LANES)
                    ],
                    axis=1,
                )

            pre = contract(edges, w1_ref[:width, :], ((1,), (0,)))
            pre = pre + contract(
                one_hot(send_col_ref[rows, :], table_rows), sender_table[...], ((1,), (0,))
            )
            pre = pre + contract(
                one_hot(recv_col_ref[rows, :], node_rows), receiver_table[...], ((1,), (0,))
            )
            hidden = silu(pre + b1_ref[...]).astype(BF16)
            update = normed(contract(hidden, w2_ref[...], ((1,), (0,))), gain_ref[...])
            spot = lax.broadcasted_iota(jnp.int32, (TILE, 1), 0) + t * TILE
            update = jnp.where(spot < count, update, 0.0).astype(BF16)
            out_buf[rows, :] = (edges.astype(F32) + update.astype(F32)).astype(BF16)
            node = lax.broadcasted_iota(jnp.int32, (node_rows, TILE), 0)
            member = jnp.where(node == recv_row_ref[:, rows], 1.0, 0.0).astype(BF16)
            messages[...] += contract(member, update, ((1,), (0,)))

        @pl.when(count <= t * TILE)
        def _():
            out_buf[rows, :] = edges_buf[rows, :]

        store(t).start()

    node_pre = contract(nodes, v1_ref[:width, :], ((1,), (0,)))
    node_pre = node_pre + contract(
        messages[...].astype(BF16), v1_ref[width:, :], ((1,), (0,))
    )
    node_hidden = silu(node_pre + c1_ref[...]).astype(BF16)
    node_out = normed(contract(node_hidden, v2_ref[...], ((1,), (0,))), node_gain_ref[...])
    new_nodes_ref[...] = (nodes.astype(F32) + node_out).astype(BF16)
    for t in range(tiles):
        store(t).wait()


def passed_along(block, axis, distance):
    devices = range(lax.axis_size(axis))
    route = [(i - distance, i) for i in devices if i - distance in devices]
    return lax.ppermute(block, axis, route)


def local(
    nodes,
    edges,
    senders,
    receivers,
    edge_count,
    send_index,
    rim_index,
    edge_w1,
    edge_b1,
    edge_w2,
    edge_gain,
    node_w1,
    node_b1,
    node_w2,
    node_gain,
):
    node_rows, width = nodes.shape
    edge_rows = edges.shape[0]
    n_lon, halo = send_index.shape
    rim = rim_index.shape[1]
    halo_out, up, down = pl.pallas_call(
        pick_kernel,
        out_shape=(
            jax.ShapeDtypeStruct((n_lon * halo, width), BF16),
            jax.ShapeDtypeStruct((rim, width), BF16),
            jax.ShapeDtypeStruct((rim, width), BF16),
        ),
        name="pick",
    )(nodes, send_index, rim_index)
    below = passed_along(up, "lat", 1)
    above = passed_along(down, "lat", -1)
    halo_in = lax.all_to_all(halo_out, "lon", 0, 0, tiled=True)
    tiles = edge_rows // TILE
    vmem = pl.BlockSpec(memory_space=pltpu.VMEM)
    new_nodes, new_edges = pl.pallas_call(
        main_kernel,
        in_specs=[pl.BlockSpec(memory_space=pltpu.SMEM)]
        + [vmem] * 15
        + [pl.BlockSpec(memory_space=pl.ANY)],
        out_specs=(vmem, pl.BlockSpec(memory_space=pl.ANY)),
        out_shape=(
            jax.ShapeDtypeStruct((node_rows, width), BF16),
            jax.ShapeDtypeStruct((edge_rows, width), BF16),
        ),
        scratch_shapes=[
            pltpu.VMEM((edge_rows, width), BF16),
            pltpu.VMEM((edge_rows, width), BF16),
            pltpu.VMEM((node_rows + n_lon * halo + 2 * rim, width), BF16),
            pltpu.VMEM((node_rows, width), BF16),
            pltpu.VMEM((node_rows, width), F32),
            pltpu.SemaphoreType.DMA((tiles,)),
            pltpu.SemaphoreType.DMA((tiles,)),
        ],
        compiler_params=pltpu.CompilerParams(vmem_limit_bytes=32 * 1024 * 1024),
        name="edges_and_nodes",
    )(
        edge_count,
        nodes,
        halo_in,
        below,
        above,
        senders.reshape(edge_rows, 1),
        receivers.reshape(edge_rows, 1),
        receivers.reshape(1, edge_rows),
        edge_w1,
        edge_b1.reshape(1, width),
        edge_w2,
        edge_gain.reshape(1, width),
        node_w1,
        node_b1.reshape(1, width),
        node_w2,
        node_gain.reshape(1, width),
        edges,
    )
    return (new_nodes, new_edges)


def solution(mesh):
    return jax.shard_map(
        local,
        mesh=mesh,
        in_specs=(
            P(("lat", "lon"), None),
            P(("lat", "lon"), None),
            P(("lat", "lon")),
            P(("lat", "lon")),
            P(("lat", "lon")),
            P(("lat", "lon"), None),
            P(("lat", "lon"), None),
            P(),
            P(),
            P(),
            P(),
            P(),
            P(),
            P(),
            P(),
        ),
        out_specs=(P(("lat", "lon"), None), P(("lat", "lon"), None)),
        check_vma=False,
    )
```

time: 116 us -> 47.3 us (0.41)
  local copies, waits for them, and re-layouts: 37.6 us -> 8.95 us
  blocking collectives: 26.2 us -> 0 us
  matrix products: 15 us -> 0 us
  between operations: 15 us -> 1.4 us
  Pallas kernels: 0 us -> 13.2 us
  starting transfers between devices: 16.2 us -> 23 us
  other arithmetic: 4.73 us -> 0 us
    gather x5 -> x0, local copies, waits for them, and re-layouts: 30.4 us -> none  [the longest x1 13 us: local(): nodes[receivers]]
    all_gather x1 -> x0, blocking collectives: 26.2 us -> none  [local(): lax.all_gather(send_index, 'lon', axis=0, tiled=True)]
    dot_general x6 -> x0, matrix products: 15 us -> none  [the longest x1 4.11 us: local(): jnp.dot(table[senders], edge_w1[width:2 * width], preferred_element_type=...]
    pallas_call x0 -> x2, Pallas kernels: none -> 13.2 us  [the longest x1 11.2 us: local(): pl.pallas_call(main_kernel, in_specs=[pl.BlockSpec(memory_space=pltpu.SME...]
    all_to_all x0 -> x1, starting transfers between devices: none -> 7.1 us  [local(): halo_in = lax.all_to_all(halo_out, 'lon', 0, 0, tiled=True)]
    convert_element_type x2 -> x0, other arithmetic: 2.67 us -> none  [the longest x1 1.88 us: local(): (edges.astype(jnp.float32) + update.astype(jnp.float32)).astype(jnp.bfloa...]
    reshape x0 -> x2, local copies, waits for them, and re-layouts: none -> 1.74 us  [the longest x1 1.24 us: local(): senders.reshape(edge_rows, 1)]
    unnamed x26 -> x22, local copies, waits for them, and re-layouts: 7.15 us -> 7.21 us
  transfers between devices with their start and end apart: 3 -> 3, of which waited for: 0 -> 0; matrix products, arithmetic and copies ran while one was open for 23% -> 4% of each run, Pallas kernels for 0% -> 0%
where the time goes in v1:
time: 47.3 us; the launch traced here: 46.6 us
  starting transfers between devices  23 us (49%)
  Pallas kernels  13.2 us (28%)
  local copies, waits for them, and re-layouts  8.95 us (19%)
  between operations  1.4 us (3%)
    ppermute x2, starting transfers between devices, passed_along(): return lax.ppermute(block, axis, route)  15.9 us
    pallas_call x1, Pallas kernels, local(): pl.pallas_call(main_kernel, in_specs=[pl.BlockSpec(memory_space=pltpu.SME...  11.2 us
    unnamed x22, local copies, waits for them, and re-layouts  7.21 us
    all_to_all x1, starting transfers between devices, local(): halo_in = lax.all_to_all(halo_out, 'lon', 0, 0, tiled=True)  7.1 us
    pallas_call x1, Pallas kernels, local(): pl.pallas_call(pick_kernel, out_shape=(jax.ShapeDtypeStruct((n_lon * halo...  2.02 us
    reshape x1, local copies, waits for them, and re-layouts, local(): senders.reshape(edge_rows, 1)  1.24 us
  transfers between devices with their start and end apart: 3, of which 0 were waited for; matrix products, arithmetic and copies ran while one was open for 4% of the time, Pallas kernels for 0%

profile of v1, /device:TPU:6, one launch (start us, length us, event | category | flops | bytes accessed | tf_op | source)
XLA Modules:
  0.0 46.6 jit_solution(1687538761699796383)
XLA Ops:
  0.6 0.0 copy-start.6
  0.6 2.0 %pick.1 = (bf16[512,256]{1,0:T(8,128)(2,1)}, bf16[128,256]{1,0:T(8,128)(2,1)}, bf16[128,256]{1,0:T(8,128)(2,1)}) custom-call(bf16[256,256]{1,0:T(8,128)(2,1)} %nodes_ref.3, s32[8,64]{1,0:T(8,128)} %send_ref.1, s32[2,128]{1,0:T(2,128)} %rim_ref.1), custom_call_target="tpu_custom_call" | custom-call | tf_op jit(solution)/shard_map/pick/pallas_call | solution.py:190
  2.7 7.1 %all-to-all-start = ((bf16[8,64,256]{2,1,0:T(8,128)(2,1)}), bf16[8,64,256]{2,1,0:T(8,128)(2,1)S(1)}, u32[]{:S(2)}, u32[]{:S(2)}) async-start(bf16[8,64,256]{2,1,0:T(8,128)(2,1)} %bitcast.16), calls=%async_computation | async-start | bytes 524288 | tf_op jit(solution)/shard_map/all_to_all | solution.py:201
  9.8 1.9 %collective-permute-start = (bf16[128,256]{1,0:T(8,128)(2,1)}, bf16[128,256]{1,0:T(8,128)(2,1)}, u32[]{:S(2)}, u32[]{:S(2)}) collective-permute-start(bf16[128,256]{1,0:T(8,128)(2,1)} %get-tuple-element.6), channel_id=1, source_target_pairs={{0,8},{8,16},{16,24},{24,32},{32,40},{40,48},{48,56},{56,64},{64,7... | collective-permute-start | bytes 196616 | tf_op jit(solution)/shard_map/ppermute | solution.py:166
  11.7 14.0 %collective-permute-start.1 = (bf16[128,256]{1,0:T(8,128)(2,1)}, bf16[128,256]{1,0:T(8,128)(2,1)}, u32[]{:S(2)}, u32[]{:S(2)}) collective-permute-start(bf16[128,256]{1,0:T(8,128)(2,1)} %get-tuple-element.7), channel_id=1, source_target_pairs={{8,0},{16,8},{24,16},{32,24},{40,32},{48,40},{56,48},{64,56},{72,6... | collective-permute-start | bytes 196616 | tf_op jit(solution)/shard_map/ppermute | solution.py:166
  26.3 0.0 copy-start.1
  26.4 0.0 copy-start.7
  26.4 1.2 %copy.17.send_col_ref = s32[3072,1]{1,0:T(8,128)S(1)} copy(s32[3072,1]{0,1:T(1,128)} %bitcast.17) | data formatting | bytes 24576 | tf_op jit(solution)/shard_map/reshape | solution.py:231
  27.6 0.0 copy-done.6
  27.6 0.5 %copy.18.recv_col_ref = s32[3072,1]{1,0:T(8,128)S(1)} copy(s32[3072,1]{0,1:T(1,128)S(1)} %bitcast.10) | data formatting | bytes 24576 | tf_op jit(solution)/shard_map/reshape | solution.py:232
  28.1 0.0 collective-permute-done.below_ref
  28.1 0.0 collective-permute-done.1.above_ref
  28.2 0.0 all-to-all-done
  28.2 0.0 copy-done.1
  28.2 0.0 copy-done.7
  28.2 0.0 copy-start
  28.2 1.4 %copy-done = bf16[3072,256]{1,0:T(8,128)(2,1)S(1)} copy-done((bf16[3072,256]{1,0:T(8,128)(2,1)S(1)}, bf16[3072,256]{1,0:T(8,128)(2,1)}, u32[]{:S(2)}) %copy-start) | copy-done | bytes 1572888
  29.6 0.0 copy-start.2
  29.6 1.0 %copy-done.2 = bf16[768,256]{1,0:T(8,128)(2,1)S(1)} copy-done((bf16[768,256]{1,0:T(8,128)(2,1)S(1)}, bf16[768,256]{1,0:T(8,128)(2,1)}, u32[]{:S(2)}) %copy-start.2) | copy-done | bytes 393240
  30.6 0.0 copy-start.3
  30.6 0.9 %copy-done.3 = bf16[512,256]{1,0:T(8,128)(2,1)S(1)} copy-done((bf16[512,256]{1,0:T(8,128)(2,1)S(1)}, bf16[512,256]{1,0:T(8,128)(2,1)}, u32[]{:S(2)}) %copy-start.3) | copy-done | bytes 262168
  31.5 0.0 copy-start.4
  31.5 0.9 %copy-done.4 = bf16[256,256]{1,0:T(8,128)(2,1)S(1)} copy-done((bf16[256,256]{1,0:T(8,128)(2,1)S(1)}, bf16[256,256]{1,0:T(8,128)(2,1)}, u32[]{:S(2)}) %copy-start.4) | copy-done | bytes 131096
  32.5 0.0 copy-start.5
  32.5 0.9 %copy-done.5 = bf16[256,256]{1,0:T(8,128)(2,1)S(1)} copy-done((bf16[256,256]{1,0:T(8,128)(2,1)S(1)}, bf16[256,256]{1,0:T(8,128)(2,1)}, u32[]{:S(2)}) %copy-start.5) | copy-done | bytes 131096
  33.4 0.0 copy-start.8
  33.4 0.7 %copy-done.8 = f32[256]{0:T(256)S(1)} copy-done((f32[256]{0:T(256)S(1)}, f32[256]{0:T(256)}, u32[]{:S(2)}) %copy-start.8) | copy-done | bytes 1048
  34.0 0.0 copy-start.9
  34.0 0.7 %copy-done.9 = f32[256]{0:T(256)S(1)} copy-done((f32[256]{0:T(256)S(1)}, f32[256]{0:T(256)}, u32[]{:S(2)}) %copy-start.9) | copy-done | bytes 1048
  34.7 0.0 copy-start.10
  34.7 0.7 %copy-done.10 = f32[256]{0:T(256)S(1)} copy-done((f32[256]{0:T(256)S(1)}, f32[256]{0:T(256)}, u32[]{:S(2)}) %copy-start.10) | copy-done | bytes 1048
  35.4 11.2 %edges_and_nodes.1 = (bf16[256,256]{1,0:T(8,128)(2,1)}, bf16[3072,256]{1,0:T(8,128)(2,1)}) custom-call(s32[1]{0:T(128)S(6)} %copy.19.count_ref, bf16[256,256]{1,0:T(8,128)(2,1)S(1)} %copy-done.1, bf16[512,256]{1,0:T(8,128)(2,1)S(1)} %bitcast.9, bf16[128,256]{1,0:T(8,128)(2,1)} %collective-permute-done.below_ref, ...), custom_call_target="tpu_custom_call" | custom-call | tf_op jit(solution)/shard_map/edges_and_nodes/pallas_call | solution.py:204
Async XLA Ops:
  0.6 27.0 %copy-start.6 = (s32[3072]{0:T(1024)S(1)}, s32[3072]{0:T(1024)}, u32[]{:S(2)}) copy-start(s32[3072]{0:T(1024)} %param.18) | copy-start | bytes 36868
  2.7 25.5 %all-to-all-start = ((bf16[8,64,256]{2,1,0:T(8,128)(2,1)}), bf16[8,64,256]{2,1,0:T(8,128)(2,1)S(1)}, u32[]{:S(2)}, u32[]{:S(2)}) async-start(bf16[8,64,256]{2,1,0:T(8,128)(2,1)} %bitcast.16), calls=%async_computation | async-start | bytes 524288 | tf_op jit(solution)/shard_map/all_to_all | solution.py:201
  9.8 18.4 %collective-permute-start = (bf16[128,256]{1,0:T(8,128)(2,1)}, bf16[128,256]{1,0:T(8,128)(2,1)}, u32[]{:S(2)}, u32[]{:S(2)}) collective-permute-start(bf16[128,256]{1,0:T(8,128)(2,1)} %get-tuple-element.6), channel_id=1, source_target_pairs={{0,8},{8,16},{16,24},{24,32},{32,40},{40,48},{48,56},{56,64},{64,7... | collective-permute-start | bytes 196616 | tf_op jit(solution)/shard_map/ppermute | solution.py:166
  11.7 16.5 %collective-permute-start.1 = (bf16[128,256]{1,0:T(8,128)(2,1)}, bf16[128,256]{1,0:T(8,128)(2,1)}, u32[]{:S(2)}, u32[]{:S(2)}) collective-permute-start(bf16[128,256]{1,0:T(8,128)(2,1)} %get-tuple-element.7), channel_id=1, source_target_pairs={{8,0},{16,8},{24,16},{32,24},{40,32},{48,40},{56,48},{64,56},{72,6... | collective-permute-start | bytes 196616 | tf_op jit(solution)/shard_map/ppermute | solution.py:166
  26.3 1.8 %copy-start.1 = (bf16[256,256]{1,0:T(8,128)(2,1)S(1)}, bf16[256,256]{1,0:T(8,128)(2,1)}, u32[]{:S(2)}) copy-start(bf16[256,256]{1,0:T(8,128)(2,1)} %nodes_ref.3) | copy-start | bytes 393220
  26.4 1.8 %copy-start.7 = (f32[256]{0:T(256)S(1)}, f32[256]{0:T(256)}, u32[]{:S(2)}) copy-start(f32[256]{0:T(256)} %param.23) | copy-start | bytes 3076
  28.2 1.4 %copy-start = (bf16[3072,256]{1,0:T(8,128)(2,1)S(1)}, bf16[3072,256]{1,0:T(8,128)(2,1)}, u32[]{:S(2)}) copy-start(bf16[3072,256]{1,0:T(8,128)(2,1)} %edges_hbm.1) | copy-start | bytes 4718596
  29.6 1.0 %copy-start.2 = (bf16[768,256]{1,0:T(8,128)(2,1)S(1)}, bf16[768,256]{1,0:T(8,128)(2,1)}, u32[]{:S(2)}) copy-start(bf16[768,256]{1,0:T(8,128)(2,1)} %w1_ref.1) | copy-start | bytes 1179652
  30.6 0.9 %copy-start.3 = (bf16[512,256]{1,0:T(8,128)(2,1)S(1)}, bf16[512,256]{1,0:T(8,128)(2,1)}, u32[]{:S(2)}) copy-start(bf16[512,256]{1,0:T(8,128)(2,1)} %v1_ref.1) | copy-start | bytes 786436
  31.5 0.9 %copy-start.4 = (bf16[256,256]{1,0:T(8,128)(2,1)S(1)}, bf16[256,256]{1,0:T(8,128)(2,1)}, u32[]{:S(2)}) copy-start(bf16[256,256]{1,0:T(8,128)(2,1)} %w2_ref.1) | copy-start | bytes 393220
  32.5 0.9 %copy-start.5 = (bf16[256,256]{1,0:T(8,128)(2,1)S(1)}, bf16[256,256]{1,0:T(8,128)(2,1)}, u32[]{:S(2)}) copy-start(bf16[256,256]{1,0:T(8,128)(2,1)} %v2_ref.1) | copy-start | bytes 393220
  33.4 0.7 %copy-start.8 = (f32[256]{0:T(256)S(1)}, f32[256]{0:T(256)}, u32[]{:S(2)}) copy-start(f32[256]{0:T(256)} %param.25) | copy-start | bytes 3076
  34.0 0.7 %copy-start.9 = (f32[256]{0:T(256)S(1)}, f32[256]{0:T(256)}, u32[]{:S(2)}) copy-start(f32[256]{0:T(256)} %param.27) | copy-start | bytes 3076
  34.7 0.7 %copy-start.10 = (f32[256]{0:T(256)S(1)}, f32[256]{0:T(256)}, u32[]{:S(2)}) copy-start(f32[256]{0:T(256)} %param.29) | copy-start | bytes 3076

commit v2 on v0

v2 whole, which is shorter than its diff:
```python
import jax
import jax.numpy as jnp
from jax import lax
from jax.experimental import pallas as pl
from jax.experimental.pallas import tpu as pltpu
from jax.sharding import PartitionSpec as P

F32 = jnp.float32
BF16 = jnp.bfloat16
I16 = jnp.int16
I32 = jnp.int32
LANES = 128
NODE_ROWS = 256
WIDTH = 256
EDGE_ROWS = 3072
N_LON = 8
HALO = 64
RIM = 128
HALO_ROWS = N_LON * HALO
REMOTE = HALO_ROWS + 2 * RIM
GROUPS = EDGE_ROWS // LANES
LOCAL_TILE = 1024
LOCAL_TILES = EDGE_ROWS // LOCAL_TILE
TILE = 1024
TILES = EDGE_ROWS // TILE
SHELF = 24
W_S, W_2, V_1, V_2 = 0, 256, 512, 1024
GAIN, C_1, NODE_GAIN = 0, 1, 2


def dot(a, b):
    return jnp.dot(a, b, preferred_element_type=F32)


def silu(x):
    half = 0.5 * x
    return half + half * jnp.tanh(half)


def normed(values, gain, live=None):
    mean = jnp.mean(values, axis=-1, keepdims=True)
    centred = values - mean
    var = jnp.mean(centred * centred, axis=-1, keepdims=True)
    scale = lax.rsqrt(var + 1e-05)
    if live is not None:
        scale = jnp.where(live, scale, 0.0)
    return centred * scale * gain


def waits_long():
    lat, lon = lax.axis_index("lat"), lax.axis_index("lon")
    return (lat + lon > 0) & (lax.rem(lat, SHELF) <= 1)


def odd_band():
    return lax.rem(lax.axis_index("lat"), 2)


def local_part(hbm, state, scratch):
    nodes_hbm, senders_hbm, receivers_hbm, edges_hbm, w1_hbm, b1_hbm, w2_hbm, v1_hbm, v2_hbm = hbm[:9]
    gain_hbm, c1_hbm, node_gain_hbm = hbm[9:]
    partial, columns, weights, vectors, receivers = state
    nodes, senders, edges, w1, b1, near_sem, far_sem, edge_sems = scratch

    near = [
        pltpu.make_async_copy(*pair, near_sem.at[i])
        for i, pair in enumerate(
            (
                (nodes_hbm, nodes),
                (senders_hbm, senders),
                (receivers_hbm, receivers),
                (w1_hbm, w1),
                (b1_hbm, b1),
            )
        )
    ]
    far = [
        pltpu.make_async_copy(*pair, far_sem.at[i])
        for i, pair in enumerate(
            (
                (w1_hbm.at[pl.ds(WIDTH, WIDTH)], weights.at[pl.ds(W_S, WIDTH)]),
                (w2_hbm, weights.at[pl.ds(W_2, WIDTH)]),
                (v1_hbm, weights.at[pl.ds(V_1, 2 * WIDTH)]),
                (v2_hbm, weights.at[pl.ds(V_2, WIDTH)]),
                (gain_hbm, vectors.at[pl.ds(GAIN, 1)]),
                (c1_hbm, vectors.at[pl.ds(C_1, 1)]),
                (node_gain_hbm, vectors.at[pl.ds(NODE_GAIN, 1)]),
            )
        )
    ]
    loads = [
        pltpu.make_async_copy(
            edges_hbm.at[pl.ds(t * LOCAL_TILE, LOCAL_TILE)],
            edges.at[pl.ds(t * LOCAL_TILE, LOCAL_TILE)],
            edge_sems.at[t],
        )
        for t in range(LOCAL_TILES)
    ]
    for copy in near + loads + far:
        copy.start()
    for copy in near:
        copy.wait()
    own = nodes[...]
    stack = jnp.concatenate(
        [
            w1[:WIDTH, :],
            dot(own, w1[WIDTH : 2 * WIDTH, :]).astype(BF16),
            dot(own, w1[2 * WIDTH :, :]).astype(BF16),
        ],
        axis=0,
    )
    lane = lax.broadcasted_iota(I32, (LANES, LANES), 1)

    def one_hot(column):
        return jnp.concatenate(
            [
                jnp.where(column == lane + j, 1.0, 0.0).astype(BF16)
                for j in range(0, NODE_ROWS, LANES)
            ],
            axis=1,
        )

    for t in range(LOCAL_TILES):
        rows = slice(t * LOCAL_TILE, (t + 1) * LOCAL_TILE)
        loads[t].wait()
        picks = []
        for g in range(t * LOCAL_TILE // LANES, (t + 1) * LOCAL_TILE // LANES):
            sender = jnp.broadcast_to(senders[g : g + 1, :], (LANES, LANES)).T
            receiver = jnp.broadcast_to(receivers[g : g + 1, :], (LANES, LANES)).T
            columns[g * LANES : (g + 1) * LANES, :] = (sender - NODE_ROWS).astype(I16)
            picks.append(jnp.concatenate([one_hot(sender), one_hot(receiver)], axis=1))
        left = jnp.concatenate([edges[rows, :], jnp.concatenate(picks, axis=0)], axis=1)
        partial[rows, :] = (dot(left, stack) + b1[...]).astype(BF16)
    for copy in far:
        copy.wait()


def pick_kernel(nodes, send_index, rim_index, *refs):
    hbm, (halo, outward, inward), state, scratch = refs[:12], refs[12:15], refs[15:20], refs[20:]
    own = nodes[...]

    def picked(row):
        spots = lax.broadcasted_iota(I32, (NODE_ROWS, row.shape[1]), 0)
        hot = jnp.where(spots == row, 1.0, 0.0).astype(BF16)
        return lax.dot_general(
            hot, own, (((0,), (0,)), ((), ())), preferred_element_type=F32
        ).astype(BF16)

    for p in range(0, N_LON, 2):
        pair = jnp.concatenate([send_index[p : p + 1, :], send_index[p + 1 : p + 2, :]], axis=1)
        halo[p * HALO : (p + 2) * HALO, :] = picked(pair)
    odd = odd_band()
    outward[...] = picked(rim_index[pl.ds(1 - odd, 1), :])
    inward[...] = picked(rim_index[pl.ds(odd, 1), :])

    @pl.when(waits_long())
    def _():
        local_part(hbm, state, scratch)


def local_kernel(*refs):
    hbm, state, scratch = refs[:12], refs[17:22], refs[22:]

    @pl.when(jnp.logical_not(waits_long()))
    def _():
        local_part(hbm, state, scratch)


def finish_kernel(
    halo,
    outward,
    inward,
    partial,
    columns,
    weights,
    vectors,
    receivers,
    count_hbm,
    nodes_hbm,
    edges_hbm,
    new_nodes,
    new_edges_hbm,
    table,
    edges,
    nodes,
    count_smem,
    in_sems,
    edge_sems,
    out_sems,
):
    first = [
        pltpu.make_async_copy(count_hbm, count_smem, in_sems.at[0]),
        pltpu.make_async_copy(nodes_hbm, nodes, in_sems.at[1]),
    ]
    loads = [
        pltpu.make_async_copy(
            edges_hbm.at[pl.ds(t * TILE, TILE)], edges.at[pl.ds(t * TILE, TILE)], edge_sems.at[t]
        )
        for t in range(TILES)
    ]
    stores = [
        pltpu.make_async_copy(
            edges.at[pl.ds(t * TILE, TILE)], new_edges_hbm.at[pl.ds(t * TILE, TILE)], out_sems.at[t]
        )
        for t in range(TILES)
    ]
    for copy in first + loads:
        copy.start()
    w_s = weights[W_S : W_S + WIDTH, :]
    odd = odd_band()
    table[:HALO_ROWS, :] = dot(halo[...], w_s).astype(BF16)
    above_even = HALO_ROWS + RIM
    from_out = pl.multiple_of(HALO_ROWS + RIM * odd, RIM)
    from_in = pl.multiple_of(above_even - RIM * odd, RIM)
    table[pl.ds(from_out, RIM), :] = dot(outward[...], w_s).astype(BF16)
    table[pl.ds(from_in, RIM), :] = dot(inward[...], w_s).astype(BF16)
    w2 = weights[W_2 : W_2 + WIDTH, :]
    gain = vectors[GAIN : GAIN + 1, :]
    remote = table[...]
    lane = lax.broadcasted_iota(I16, (TILE, LANES), 1)
    one, zero = jnp.ones((), BF16), jnp.zeros((), BF16)
    node = lax.broadcasted_iota(I32, (NODE_ROWS, LANES), 0)
    for copy in first:
        copy.wait()
    count = count_smem[0]
    messages = jnp.zeros((NODE_ROWS, WIDTH), F32)

    for t in range(TILES):
        rows = slice(t * TILE, (t + 1) * TILE)
        column = columns[rows, :]
        chosen = jnp.concatenate(
            [jnp.where(column == lane + j, one, zero) for j in range(0, REMOTE, LANES)], axis=1
        )
        pre = partial[rows, :].astype(F32) + dot(chosen, remote)
        spot = lax.broadcasted_iota(I32, (TILE, 1), 0) + t * TILE
        update = normed(dot(silu(pre).astype(BF16), w2), gain, spot < count).astype(BF16)
        loads[t].wait()
        edges[rows, :] = (edges[rows, :].astype(F32) + update.astype(F32)).astype(BF16)
        stores[t].start()
        member = jnp.concatenate(
            [
                jnp.where(node == receivers[g : g + 1, :], 1.0, 0.0).astype(BF16)
                for g in range(t * TILE // LANES, (t + 1) * TILE // LANES)
            ],
            axis=1,
        )
        messages = messages + dot(member, update)

    own = nodes[...]
    both = jnp.concatenate([own, messages.astype(BF16)], axis=1)
    v1 = weights[V_1 : V_1 + 2 * WIDTH, :]
    node_hidden = silu(dot(both, v1) + vectors[C_1 : C_1 + 1, :]).astype(BF16)
    node_out = normed(
        dot(node_hidden, weights[V_2 : V_2 + WIDTH, :]), vectors[NODE_GAIN : NODE_GAIN + 1, :]
    )
    new_nodes[...] = (own.astype(F32) + node_out).astype(BF16)
    for copy in stores:
        copy.wait()


def in_hbm(x):
    return pltpu.with_memory_space_constraint(x, pltpu.HBM)


def in_vmem(x):
    return pltpu.with_memory_space_constraint(x, pltpu.VMEM)


def local(
    nodes,
    edges,
    senders,
    receivers,
    edge_count,
    send_index,
    rim_index,
    edge_w1,
    edge_b1,
    edge_w2,
    edge_gain,
    node_w1,
    node_b1,
    node_w2,
    node_gain,
):
    vmem = pl.BlockSpec(memory_space=pltpu.VMEM)
    hbm = pl.BlockSpec(memory_space=pltpu.HBM)
    params = pltpu.CompilerParams(vmem_limit_bytes=12 * 1024 * 1024)
    groups = (GROUPS, LANES)
    nodes, edges = map(in_hbm, (nodes, edges))
    far = tuple(
        map(
            in_hbm,
            (
                nodes,
                senders.reshape(groups),
                receivers.reshape(groups),
                edges,
                edge_w1,
                edge_b1.reshape(1, WIDTH),
                edge_w2,
                node_w1,
                node_w2,
                edge_gain.reshape(1, WIDTH),
                node_b1.reshape(1, WIDTH),
                node_gain.reshape(1, WIDTH),
            ),
        )
    )
    state_shape = (
        pltpu.VMEM((EDGE_ROWS, WIDTH), BF16),
        pltpu.VMEM((EDGE_ROWS, LANES), I16),
        pltpu.VMEM((5 * WIDTH, WIDTH), BF16),
        pltpu.VMEM((8, WIDTH), F32),
        pltpu.VMEM(groups, I32),
    )
    scratch = [
        pltpu.VMEM((NODE_ROWS, WIDTH), BF16),
        pltpu.VMEM(groups, I32),
        pltpu.VMEM((EDGE_ROWS, WIDTH), BF16),
        pltpu.VMEM((3 * WIDTH, WIDTH), BF16),
        pltpu.VMEM((1, WIDTH), F32),
        pltpu.SemaphoreType.DMA((5,)),
        pltpu.SemaphoreType.DMA((7,)),
        pltpu.SemaphoreType.DMA((LOCAL_TILES,)),
    ]
    halo, outward, inward, *state = pl.pallas_call(
        pick_kernel,
        in_specs=[vmem] * 3 + [hbm] * 12,
        out_specs=[vmem] * 8,
        out_shape=(
            jax.ShapeDtypeStruct((HALO_ROWS, WIDTH), BF16),
            jax.ShapeDtypeStruct((RIM, WIDTH), BF16),
            jax.ShapeDtypeStruct((RIM, WIDTH), BF16),
        )
        + state_shape,
        scratch_shapes=scratch,
        compiler_params=params,
        name="pick_rows",
    )(nodes, in_hbm(send_index), in_hbm(rim_index), *far)
    halo = lax.all_to_all(halo, "lon", 0, 0, tiled=True)
    bands = lax.axis_size("lat")
    outward = lax.ppermute(
        outward, "lat", [(i, ((i + 1) ^ 1) - 1) for i in range(1, bands - 1)]
    )
    inward = lax.ppermute(inward, "lat", [(i, i ^ 1) for i in range(bands)])
    state = pl.pallas_call(
        local_kernel,
        in_specs=[hbm] * 12 + [vmem] * 5,
        out_specs=[vmem] * 5,
        out_shape=state_shape,
        input_output_aliases={12 + i: i for i in range(5)},
        scratch_shapes=scratch,
        compiler_params=params,
        cost_estimate=pl.CostEstimate(
            flops=2 * EDGE_ROWS * 3 * WIDTH * WIDTH, bytes_accessed=8_000_000, transcendentals=0
        ),
        name="local_edges",
    )(*far, *map(in_vmem, state))
    return pl.pallas_call(
        finish_kernel,
        in_specs=[vmem] * 8 + [pl.BlockSpec(memory_space=pl.ANY)] + [hbm] * 2,
        out_specs=[vmem, hbm],
        out_shape=(
            jax.ShapeDtypeStruct((NODE_ROWS, WIDTH), BF16),
            pltpu.HBM((EDGE_ROWS, WIDTH), BF16),
        ),
        scratch_shapes=[
            pltpu.VMEM((REMOTE, WIDTH), BF16),
            pltpu.VMEM((EDGE_ROWS, WIDTH), BF16),
            pltpu.VMEM((NODE_ROWS, WIDTH), BF16),
            pltpu.SMEM((1,), I32),
            pltpu.SemaphoreType.DMA((2,)),
            pltpu.SemaphoreType.DMA((TILES,)),
            pltpu.SemaphoreType.DMA((TILES,)),
        ],
        compiler_params=pltpu.CompilerParams(vmem_limit_bytes=24 * 1024 * 1024),
        name="edges_and_nodes",
    )(*map(in_vmem, (halo, outward, inward, *state)), edge_count, nodes, edges)


def solution(mesh):
    spread = P(("lat", "lon"))
    rows = P(("lat", "lon"), None)
    return jax.shard_map(
        local,
        mesh=mesh,
        in_specs=(rows, rows, spread, spread, spread, rows, rows) + (P(),) * 8,
        out_specs=(rows, rows),
        check_vma=False,
    )
```

time: 116 us -> 35.8 us (0.31)
  the two profiles are of different devices: /device:TPU:6 before, /device:TPU:15 now
where the time goes in v2:
time: 35.8 us; the launch traced here: 35.5 us
  starting transfers between devices  19.6 us (55%)
  Pallas kernels  14.6 us (41%)
  between operations  1.32 us (4%)
    ppermute x1, starting transfers between devices, local(): inward = lax.ppermute(inward, 'lat', [(i, i ^ 1) for i in range(bands)])  10.7 us
    pallas_call x1, Pallas kernels, local(): pl.pallas_call(finish_kernel, in_specs=[vmem] * 8 + [pl.BlockSpec(memory_...  7.93 us
    all_to_all x1, starting transfers between devices, local(): halo = lax.all_to_all(halo, 'lon', 0, 0, tiled=True)  6.99 us
    pallas_call x1, Pallas kernels, local(): pl.pallas_call(pick_kernel, in_specs=[vmem] * 3 + [hbm] * 12, out_specs=[...  6.45 us
    ppermute x1, starting transfers between devices, local(): lax.ppermute(outward, 'lat', [(i, (i + 1 ^ 1) - 1) for i in range(1, band...  1.91 us
  transfers between devices with their start and end apart: 3, of which 0 were waited for; matrix products, arithmetic and copies ran while one was open for 0% of the time, Pallas kernels for 0%

profile of v2, /device:TPU:15, one launch (start us, length us, event | category | flops | bytes accessed | tf_op | source)
XLA Modules:
  0.0 35.5 jit_solution(3326854497089898488)
XLA Ops:
  0.6 6.4 %pick_rows.1 = (bf16[512,256]{1,0:T(8,128)(2,1)}, bf16[128,256]{1,0:T(8,128)(2,1)}, bf16[128,256]{1,0:T(8,128)(2,1)S(1)}, bf16[3072,256]{1,0:T(8,128)(2,1)S(1)},...) custom-call(bf16[256,256]{1,0:T(8,128)(2,1)} %nodes_hbm.1, ...), custom_call_target="tpu_custom_call" | custom-call | tf_op jit(solution)/shard_map/pick_rows/pallas_call | solution.py:327
  7.1 7.0 %all-to-all-start = ((bf16[8,64,256]{2,1,0:T(8,128)(2,1)}), bf16[8,64,256]{2,1,0:T(8,128)(2,1)S(1)}, u32[]{:S(2)}, u32[]{:S(2)}) async-start(bf16[8,64,256]{2,1,0:T(8,128)(2,1)} %bitcast.6), calls=%async_computation | async-start | bytes 524288 | tf_op jit(solution)/shard_map/all_to_all | solution.py:341
  14.1 1.9 %collective-permute-start = (bf16[128,256]{1,0:T(8,128)(2,1)}, bf16[128,256]{1,0:T(8,128)(2,1)S(1)}, u32[]{:S(2)}, u32[]{:S(2)}) collective-permute-start(bf16[128,256]{1,0:T(8,128)(2,1)} %get-tuple-element.16), channel_id=1, source_target_pairs={{8,16},{16,8},{24,32},{32,24},{40,48},{48,40},{56,64},{64,56},{72,... | collective-permute-start | bytes 196616 | tf_op jit(solution)/shard_map/ppermute | solution.py:343
  16.0 10.7 %collective-permute-start.1 = (bf16[128,256]{1,0:T(8,128)(2,1)S(1)}, bf16[128,256]{1,0:T(8,128)(2,1)S(1)}, u32[]{:S(2)}, u32[]{:S(2)}) collective-permute-start(bf16[128,256]{1,0:T(8,128)(2,1)S(1)} %get-tuple-element.17), channel_id=1, source_target_pairs={{0,8},{8,0},{16,24},{24,16},{32,40},{40,32},{48,56},{56,48},{64,72... | collective-permute-start | bytes 196616 | tf_op jit(solution)/shard_map/ppermute | solution.py:346
  27.3 0.2 local_edges.1
  27.5 0.0 collective-permute-done.outward
  27.5 0.0 collective-permute-done.1.inward
  27.6 0.0 all-to-all-done
  27.6 7.9 %edges_and_nodes.1 = (bf16[256,256]{1,0:T(8,128)(2,1)}, bf16[3072,256]{1,0:T(8,128)(2,1)}) custom-call(bf16[512,256]{1,0:T(8,128)(2,1)S(1)} %bitcast.8, bf16[128,256]{1,0:T(8,128)(2,1)S(1)} %collective-permute-done.outward, bf16[128,256]{1,0:T(8,128)(2,1)S(1)} %collective-permute-done.1.inward, bf16[3072,256]{1,0:T(8,128)(2,1)S(1)} %get-tuple-element.23.partial, ...), custom_call_target="tpu_custom_call" | custom-call | tf_op jit(solution)/shard_map/edges_and_nodes/pallas_call | solution.py:360
Async XLA Ops:
  7.1 20.5 %all-to-all-start = ((bf16[8,64,256]{2,1,0:T(8,128)(2,1)}), bf16[8,64,256]{2,1,0:T(8,128)(2,1)S(1)}, u32[]{:S(2)}, u32[]{:S(2)}) async-start(bf16[8,64,256]{2,1,0:T(8,128)(2,1)} %bitcast.6), calls=%async_computation | async-start | bytes 524288 | tf_op jit(solution)/shard_map/all_to_all | solution.py:341
  14.1 13.4 %collective-permute-start = (bf16[128,256]{1,0:T(8,128)(2,1)}, bf16[128,256]{1,0:T(8,128)(2,1)S(1)}, u32[]{:S(2)}, u32[]{:S(2)}) collective-permute-start(bf16[128,256]{1,0:T(8,128)(2,1)} %get-tuple-element.16), channel_id=1, source_target_pairs={{8,16},{16,8},{24,32},{32,24},{40,48},{48,40},{56,64},{64,56},{72,... | collective-permute-start | bytes 196616 | tf_op jit(solution)/shard_map/ppermute | solution.py:343
  16.0 11.6 %collective-permute-start.1 = (bf16[128,256]{1,0:T(8,128)(2,1)S(1)}, bf16[128,256]{1,0:T(8,128)(2,1)S(1)}, u32[]{:S(2)}, u32[]{:S(2)}) collective-permute-start(bf16[128,256]{1,0:T(8,128)(2,1)S(1)} %get-tuple-element.17), channel_id=1, source_target_pairs={{0,8},{8,0},{16,24},{24,16},{32,40},{40,32},{48,56},{56,48},{64,72... | collective-permute-start | bytes 196616 | tf_op jit(solution)/shard_map/ppermute | solution.py:346

commit v3 on v2

--- a/solution.py
+++ b/solution.py
@@ -24,7 +24,7 @@
 TILE = 1024
 TILES = EDGE_ROWS // TILE
 SHELF = 24
-W_S, W_2, V_1, V_2 = 0, 256, 512, 1024
+W_S, W_2 = 0, 256
 GAIN, C_1, NODE_GAIN = 0, 1, 2
 
 
@@ -37,9 +37,12 @@
     return half + half * jnp.tanh(half)
 
 
-def normed(values, gain, live=None):
-    mean = jnp.mean(values, axis=-1, keepdims=True)
-    centred = values - mean
+def without_mean(weights):
+    wide = weights.astype(F32)
+    return (wide - jnp.mean(wide, axis=-1, keepdims=True)).astype(BF16)
+
+
+def scaled(centred, gain, live=None):
     var = jnp.mean(centred * centred, axis=-1, keepdims=True)
     scale = lax.rsqrt(var + 1e-05)
     if live is not None:
@@ -57,8 +60,8 @@
 
 
 def local_part(hbm, state, scratch):
-    nodes_hbm, senders_hbm, receivers_hbm, edges_hbm, w1_hbm, b1_hbm, w2_hbm, v1_hbm, v2_hbm = hbm[:9]
-    gain_hbm, c1_hbm, node_gain_hbm = hbm[9:]
+    nodes_hbm, senders_hbm, receivers_hbm, edges_hbm, w1_hbm, b1_hbm, w2_hbm = hbm[:7]
+    gain_hbm, c1_hbm, node_gain_hbm = hbm[7:]
     partial, columns, weights, vectors, receivers = state
     nodes, senders, edges, w1, b1, near_sem, far_sem, edge_sems = scratch
 
@@ -80,8 +83,6 @@
             (
                 (w1_hbm.at[pl.ds(WIDTH, WIDTH)], weights.at[pl.ds(W_S, WIDTH)]),
                 (w2_hbm, weights.at[pl.ds(W_2, WIDTH)]),
-                (v1_hbm, weights.at[pl.ds(V_1, 2 * WIDTH)]),
-                (v2_hbm, weights.at[pl.ds(V_2, WIDTH)]),
                 (gain_hbm, vectors.at[pl.ds(GAIN, 1)]),
                 (c1_hbm, vectors.at[pl.ds(C_1, 1)]),
                 (node_gain_hbm, vectors.at[pl.ds(NODE_GAIN, 1)]),
@@ -133,33 +134,68 @@
         partial[rows, :] = (dot(left, stack) + b1[...]).astype(BF16)
     for copy in far:
         copy.wait()
-
-
-def pick_kernel(nodes, send_index, rim_index, *refs):
-    hbm, (halo, outward, inward), state, scratch = refs[:12], refs[12:15], refs[15:20], refs[20:]
+    weights[W_2 : W_2 + WIDTH, :] = without_mean(weights[W_2 : W_2 + WIDTH, :])
+
+
+def pick_kernel(nodes_hbm, send_hbm, rim_hbm, *refs):
+    hbm, (halo_hbm, outward, inward), state, refs = refs[:10], refs[10:13], refs[13:18], refs[18:]
+    nodes, send_index, rim_index, halo, in_sems, out_sems = refs[:6]
+    into = [
+        pltpu.make_async_copy(*pair, in_sems.at[i])
+        for i, pair in enumerate(
+            ((send_hbm, send_index), (nodes_hbm, nodes), (rim_hbm, rim_index))
+        )
+    ]
+    pairs = range(N_LON // 2)
+    away = [
+        pltpu.make_async_copy(
+            halo.at[pl.ds(p * 2 * HALO, 2 * HALO)],
+            halo_hbm.at[pl.ds(p * 2 * HALO, 2 * HALO)],
+            out_sems.at[p],
+        )
+        for p in pairs
+    ]
+    for copy in into:
+        copy.start()
+
+    def hot(row):
+        spots = lax.broadcasted_iota(I32, (NODE_ROWS, row.shape[1]), 0)
+        return jnp.where(spots == row, 1.0, 0.0).astype(BF16)
+
+    def picked(chosen, own):
+        return lax.dot_general(
+            chosen, own, (((0,), (0,)), ((), ())), preferred_element_type=F32
+        ).astype(BF16)
+
+    into[0].wait()
+    chosen = [
+        hot(
+            jnp.concatenate(
+                [send_index[2 * p : 2 * p + 1, :], send_index[2 * p + 1 : 2 * p + 2, :]], axis=1
+            )
+        )
+        for p in pairs
+    ]
+    into[1].wait()
     own = nodes[...]
-
-    def picked(row):
-        spots = lax.broadcasted_iota(I32, (NODE_ROWS, row.shape[1]), 0)
-        hot = jnp.where(spots == row, 1.0, 0.0).astype(BF16)
-        return lax.dot_general(
-            hot, own, (((0,), (0,)), ((), ())), preferred_element_type=F32
-        ).astype(BF16)
-
-    for p in range(0, N_LON, 2):
-        pair = jnp.concatenate([send_index[p : p + 1, :], send_index[p + 1 : p + 2, :]], axis=1)
-        halo[p * HALO : (p + 2) * HALO, :] = picked(pair)
+    for p in pairs:
+        halo[2 * p * HALO : 2 * (p + 1) * HALO, :] = picked(chosen[p], own)
+        away[p].start()
+    into[2].wait()
     odd = odd_band()
-    outward[...] = picked(rim_index[pl.ds(1 - odd, 1), :])
-    inward[...] = picked(rim_index[pl.ds(odd, 1), :])
+    outward[...] = picked(hot(rim_index[pl.ds(1 - odd, 1), :]), own)
+    inward[...] = picked(hot(rim_index[pl.ds(odd, 1), :]), own)
 
     @pl.when(waits_long())
     def _():
-        local_part(hbm, state, scratch)
+        local_part(hbm, state, refs[6:])
+
+    for copy in away:
+        copy.wait()
 
 
 def local_kernel(*refs):
-    hbm, state, scratch = refs[:12], refs[17:22], refs[22:]
+    hbm, state, scratch = refs[:10], refs[15:20], refs[20:]
 
     @pl.when(jnp.logical_not(waits_long()))
     def _():
@@ -175,22 +211,26 @@
     weights,
     vectors,
     receivers,
-    count_hbm,
+    count_smem,
     nodes_hbm,
     edges_hbm,
-    new_nodes,
+    v1_hbm,
+    v2_hbm,
+    new_nodes_hbm,
     new_edges_hbm,
     table,
     edges,
     nodes,
-    count_smem,
+    v1,
+    v2,
     in_sems,
     edge_sems,
     out_sems,
 ):
-    first = [
-        pltpu.make_async_copy(count_hbm, count_smem, in_sems.at[0]),
-        pltpu.make_async_copy(nodes_hbm, nodes, in_sems.at[1]),
+    late = [
+        pltpu.make_async_copy(nodes_hbm, nodes, in_sems.at[0]),
+        pltpu.make_async_copy(v1_hbm, v1, in_sems.at[1]),
+        pltpu.make_async_copy(v2_hbm, v2, in_sems.at[2]),
     ]
     loads = [
         pltpu.make_async_copy(
@@ -203,15 +243,14 @@
             edges.at[pl.ds(t * TILE, TILE)], new_edges_hbm.at[pl.ds(t * TILE, TILE)], out_sems.at[t]
         )
         for t in range(TILES)
-    ]
-    for copy in first + loads:
+    ] + [pltpu.make_async_copy(nodes, new_nodes_hbm, out_sems.at[TILES])]
+    for copy in loads + late:
         copy.start()
     w_s = weights[W_S : W_S + WIDTH, :]
     odd = odd_band()
     table[:HALO_ROWS, :] = dot(halo[...], w_s).astype(BF16)
-    above_even = HALO_ROWS + RIM
     from_out = pl.multiple_of(HALO_ROWS + RIM * odd, RIM)
-    from_in = pl.multiple_of(above_even - RIM * odd, RIM)
+    from_in = pl.multiple_of(HALO_ROWS + RIM - RIM * odd, RIM)
     table[pl.ds(from_out, RIM), :] = dot(outward[...], w_s).astype(BF16)
     table[pl.ds(from_in, RIM), :] = dot(inward[...], w_s).astype(BF16)
     w2 = weights[W_2 : W_2 + WIDTH, :]
@@ -220,10 +259,8 @@
     lane = lax.broadcasted_iota(I16, (TILE, LANES), 1)
     one, zero = jnp.ones((), BF16), jnp.zeros((), BF16)
     node = lax.broadcasted_iota(I32, (NODE_ROWS, LANES), 0)
-    for copy in first:
-        copy.wait()
+    messages = jnp.zeros((NODE_ROWS, WIDTH), F32)
     count = count_smem[0]
-    messages = jnp.zeros((NODE_ROWS, WIDTH), F32)
 
     for t in range(TILES):
         rows = slice(t * TILE, (t + 1) * TILE)
@@ -233,7 +270,7 @@
         )
         pre = partial[rows, :].astype(F32) + dot(chosen, remote)
         spot = lax.broadcasted_iota(I32, (TILE, 1), 0) + t * TILE
-        update = normed(dot(silu(pre).astype(BF16), w2), gain, spot < count).astype(BF16)
+        update = scaled(dot(silu(pre).astype(BF16), w2), gain, spot < count).astype(BF16)
         loads[t].wait()
         edges[rows, :] = (edges[rows, :].astype(F32) + update.astype(F32)).astype(BF16)
         stores[t].start()
@@ -246,14 +283,16 @@
         )
         messages = messages + dot(member, update)
 
+    for copy in late:
+        copy.wait()
     own = nodes[...]
     both = jnp.concatenate([own, messages.astype(BF16)], axis=1)
-    v1 = weights[V_1 : V_1 + 2 * WIDTH, :]
-    node_hidden = silu(dot(both, v1) + vectors[C_1 : C_1 + 1, :]).astype(BF16)
-    node_out = normed(
-        dot(node_hidden, weights[V_2 : V_2 + WIDTH, :]), vectors[NODE_GAIN : NODE_GAIN + 1, :]
-    )
-    new_nodes[...] = (own.astype(F32) + node_out).astype(BF16)
+    node_hidden = silu(dot(both, v1[...]) + vectors[C_1 : C_1 + 1, :]).astype(BF16)
+    node_out = scaled(
+        dot(node_hidden, without_mean(v2[...])), vectors[NODE_GAIN : NODE_GAIN + 1, :]
+    )
+    nodes[...] = (own.astype(F32) + node_out).astype(BF16)
+    stores[TILES].start()
     for copy in stores:
         copy.wait()
 
@@ -299,8 +338,6 @@
                 edge_w1,
                 edge_b1.reshape(1, WIDTH),
                 edge_w2,
-                node_w1,
-                node_w2,
                 edge_gain.reshape(1, WIDTH),
                 node_b1.reshape(1, WIDTH),
                 node_gain.reshape(1, WIDTH),
@@ -310,7 +347,7 @@
     state_shape = (
         pltpu.VMEM((EDGE_ROWS, WIDTH), BF16),
         pltpu.VMEM((EDGE_ROWS, LANES), I16),
-        pltpu.VMEM((5 * WIDTH, WIDTH), BF16),
+        pltpu.VMEM((2 * WIDTH, WIDTH), BF16),
         pltpu.VMEM((8, WIDTH), F32),
         pltpu.VMEM(groups, I32),
     )
@@ -321,20 +358,28 @@
         pltpu.VMEM((3 * WIDTH, WIDTH), BF16),
         pltpu.VMEM((1, WIDTH), F32),
         pltpu.SemaphoreType.DMA((5,)),
-        pltpu.SemaphoreType.DMA((7,)),
+        pltpu.SemaphoreType.DMA((5,)),
         pltpu.SemaphoreType.DMA((LOCAL_TILES,)),
     ]
     halo, outward, inward, *state = pl.pallas_call(
         pick_kernel,
-        in_specs=[vmem] * 3 + [hbm] * 12,
-        out_specs=[vmem] * 8,
+        in_specs=[hbm] * 13,
+        out_specs=[hbm] + [vmem] * 7,
         out_shape=(
-            jax.ShapeDtypeStruct((HALO_ROWS, WIDTH), BF16),
-            jax.ShapeDtypeStruct((RIM, WIDTH), BF16),
-            jax.ShapeDtypeStruct((RIM, WIDTH), BF16),
+            pltpu.HBM((HALO_ROWS, WIDTH), BF16),
+            pltpu.VMEM((RIM, WIDTH), BF16),
+            pltpu.VMEM((RIM, WIDTH), BF16),
         )
         + state_shape,
-        scratch_shapes=scratch,
+        scratch_shapes=[
+            pltpu.VMEM((NODE_ROWS, WIDTH), BF16),
+            pltpu.VMEM((N_LON, HALO), I32),
+            pltpu.VMEM((2, RIM), I32),
+            pltpu.VMEM((HALO_ROWS, WIDTH), BF16),
+            pltpu.SemaphoreType.DMA((3,)),
+            pltpu.SemaphoreType.DMA((N_LON // 2,)),
+        ]
+        + scratch,
         compiler_params=params,
         name="pick_rows",
     )(nodes, in_hbm(send_index), in_hbm(rim_index), *far)
@@ -346,10 +391,10 @@
     inward = lax.ppermute(inward, "lat", [(i, i ^ 1) for i in range(bands)])
     state = pl.pallas_call(
         local_kernel,
-        in_specs=[hbm] * 12 + [vmem] * 5,
+        in_specs=[hbm] * 10 + [vmem] * 5,
         out_specs=[vmem] * 5,
         out_shape=state_shape,
-        input_output_aliases={12 + i: i for i in range(5)},
+        input_output_aliases={10 + i: i for i in range(5)},
         scratch_shapes=scratch,
         compiler_params=params,
         cost_estimate=pl.CostEstimate(
@@ -359,24 +404,29 @@
     )(*far, *map(in_vmem, state))
     return pl.pallas_call(
         finish_kernel,
-        in_specs=[vmem] * 8 + [pl.BlockSpec(memory_space=pl.ANY)] + [hbm] * 2,
-        out_specs=[vmem, hbm],
+        in_specs=[vmem] * 8 + [pl.BlockSpec(memory_space=pltpu.SMEM)] + [hbm] * 4,
+        out_specs=[hbm, hbm],
         out_shape=(
-            jax.ShapeDtypeStruct((NODE_ROWS, WIDTH), BF16),
+            pltpu.HBM((NODE_ROWS, WIDTH), BF16),
             pltpu.HBM((EDGE_ROWS, WIDTH), BF16),
         ),
         scratch_shapes=[
             pltpu.VMEM((REMOTE, WIDTH), BF16),
             pltpu.VMEM((EDGE_ROWS, WIDTH), BF16),
             pltpu.VMEM((NODE_ROWS, WIDTH), BF16),
-            pltpu.SMEM((1,), I32),
-            pltpu.SemaphoreType.DMA((2,)),
+            pltpu.VMEM((2 * WIDTH, WIDTH), BF16),
+            pltpu.VMEM((WIDTH, WIDTH), BF16),
+            pltpu.SemaphoreType.DMA((3,)),
             pltpu.SemaphoreType.DMA((TILES,)),
-            pltpu.SemaphoreType.DMA((TILES,)),
+            pltpu.SemaphoreType.DMA((TILES + 1,)),
         ],
         compiler_params=pltpu.CompilerParams(vmem_limit_bytes=24 * 1024 * 1024),
         name="edges_and_nodes",
-    )(*map(in_vmem, (halo, outward, inward, *state)), edge_count, nodes, edges)
+    )(
+        *map(in_vmem, (halo, outward, inward, *state)),
+        edge_count,
+        *map(in_hbm, (nodes, edges, node_w1, node_w2)),
+    )
 
 
 def solution(mesh):

time: 35.8 us -> 34.1 us (0.953)
  Pallas kernels: 14.6 us -> 12.4 us
    pallas_call x1, Pallas kernels: 7.93 us -> 6.36 us  [local(): pl.pallas_call(finish_kernel, in_specs=[vmem] * 8 + [pl.BlockSpec(memory_...]
    pallas_call x2, Pallas kernels: 6.62 us -> 6.08 us  [the longest x1 5.93 us: local(): pl.pallas_call(pick_kernel, in_specs=[hbm] * 13, out_specs=[hbm] + [vmem]...]
  transfers between devices with their start and end apart: 3 -> 3, of which waited for: 0 -> 1; matrix products, arithmetic and copies ran while one was open for 0% -> 0% of each run, Pallas kernels for 0% -> 0%
where the time goes in v3:
time: 34.1 us; the launch traced here: 33.8 us
  starting transfers between devices  19.9 us (58%)
  Pallas kernels  12.4 us (36%)
  between operations  1.32 us (4%)
    ppermute x1, starting transfers between devices, local(): inward = lax.ppermute(inward, 'lat', [(i, i ^ 1) for i in range(bands)])  11 us
    all_to_all x1, starting transfers between devices, local(): halo = lax.all_to_all(halo, 'lon', 0, 0, tiled=True)  7 us
    pallas_call x1, Pallas kernels, local(): pl.pallas_call(finish_kernel, in_specs=[vmem] * 8 + [pl.BlockSpec(memory_...  6.36 us
    pallas_call x1, Pallas kernels, local(): pl.pallas_call(pick_kernel, in_specs=[hbm] * 13, out_specs=[hbm] + [vmem]...  5.93 us
    ppermute x1, starting transfers between devices, local(): lax.ppermute(outward, 'lat', [(i, (i + 1 ^ 1) - 1) for i in range(1, band...  1.91 us
  transfers between devices with their start and end apart: 3, of which 1 were waited for; matrix products, arithmetic and copies ran while one was open for 0% of the time, Pallas kernels for 0%

profile of v3, /device:TPU:15, one launch (start us, length us, event | category | flops | bytes accessed | tf_op | source)
XLA Modules:
  0.0 33.8 jit_solution(10715140982848772726)
XLA Ops:
  0.6 5.9 %pick_rows.1 = (bf16[512,256]{1,0:T(8,128)(2,1)}, bf16[128,256]{1,0:T(8,128)(2,1)S(1)}, bf16[128,256]{1,0:T(8,128)(2,1)S(1)}, bf16[3072,256]{1,0:T(8,128)(2,1)S(...) custom-call(bf16[256,256]{1,0:T(8,128)(2,1)} %nodes_hbm.3, ...), custom_call_target="tpu_custom_call" | custom-call | tf_op jit(solution)/shard_map/pick_rows/pallas_call | solution.py:364
  6.6 7.0 %all-to-all-start = ((bf16[8,64,256]{2,1,0:T(8,128)(2,1)}), bf16[8,64,256]{2,1,0:T(8,128)(2,1)S(1)}, u32[]{:S(2)}, u32[]{:S(2)}) async-start(bf16[8,64,256]{2,1,0:T(8,128)(2,1)} %bitcast.9), calls=%async_computation | async-start | bytes 524288 | tf_op jit(solution)/shard_map/all_to_all | solution.py:386
  13.6 1.9 %collective-permute-start = (bf16[128,256]{1,0:T(8,128)(2,1)S(1)}, bf16[128,256]{1,0:T(8,128)(2,1)S(1)}, u32[]{:S(2)}, u32[]{:S(2)}) collective-permute-start(bf16[128,256]{1,0:T(8,128)(2,1)S(1)} %get-tuple-element.16), channel_id=1, source_target_pairs={{8,16},{16,8},{24,32},{32,24},{40,48},{48,40},{56,64},{64,56},{72,... | collective-permute-start | bytes 196616 | tf_op jit(solution)/shard_map/ppermute | solution.py:388
  15.5 11.0 %collective-permute-start.1 = (bf16[128,256]{1,0:T(8,128)(2,1)S(1)}, bf16[128,256]{1,0:T(8,128)(2,1)S(1)}, u32[]{:S(2)}, u32[]{:S(2)}) collective-permute-start(bf16[128,256]{1,0:T(8,128)(2,1)S(1)} %get-tuple-element.17), channel_id=1, source_target_pairs={{0,8},{8,0},{16,24},{24,16},{32,40},{40,32},{48,56},{56,48},{64,72... | collective-permute-start | bytes 196616 | tf_op jit(solution)/shard_map/ppermute | solution.py:391
  27.2 0.2 local_edges.1
  27.3 0.0 collective-permute-done.outward
  27.3 0.1 collective-permute-done.1.inward
  27.4 0.0 all-to-all-done
  27.4 6.4 %edges_and_nodes.1 = (bf16[256,256]{1,0:T(8,128)(2,1)}, bf16[3072,256]{1,0:T(8,128)(2,1)}) custom-call(bf16[512,256]{1,0:T(8,128)(2,1)S(1)} %bitcast.8, bf16[128,256]{1,0:T(8,128)(2,1)S(1)} %collective-permute-done.outward, bf16[128,256]{1,0:T(8,128)(2,1)S(1)} %collective-permute-done.1.inward, bf16[3072,256]{1,0:T(8,128)(2,1)S(1)} %get-tuple-element.23.partial, ...), custom_call_target="tpu_custom_call" | custom-call | tf_op jit(solution)/shard_map/edges_and_nodes/pallas_call | solution.py:405
Async XLA Ops:
  6.6 20.8 %all-to-all-start = ((bf16[8,64,256]{2,1,0:T(8,128)(2,1)}), bf16[8,64,256]{2,1,0:T(8,128)(2,1)S(1)}, u32[]{:S(2)}, u32[]{:S(2)}) async-start(bf16[8,64,256]{2,1,0:T(8,128)(2,1)} %bitcast.9), calls=%async_computation | async-start | bytes 524288 | tf_op jit(solution)/shard_map/all_to_all | solution.py:386
  13.6 13.8 %collective-permute-start = (bf16[128,256]{1,0:T(8,128)(2,1)S(1)}, bf16[128,256]{1,0:T(8,128)(2,1)S(1)}, u32[]{:S(2)}, u32[]{:S(2)}) collective-permute-start(bf16[128,256]{1,0:T(8,128)(2,1)S(1)} %get-tuple-element.16), channel_id=1, source_target_pairs={{8,16},{16,8},{24,32},{32,24},{40,48},{48,40},{56,64},{64,56},{72,... | collective-permute-start | bytes 196616 | tf_op jit(solution)/shard_map/ppermute | solution.py:388
  15.5 11.9 %collective-permute-start.1 = (bf16[128,256]{1,0:T(8,128)(2,1)S(1)}, bf16[128,256]{1,0:T(8,128)(2,1)S(1)}, u32[]{:S(2)}, u32[]{:S(2)}) collective-permute-start(bf16[128,256]{1,0:T(8,128)(2,1)S(1)} %get-tuple-element.17), channel_id=1, source_target_pairs={{0,8},{8,0},{16,24},{24,16},{32,40},{40,32},{48,56},{56,48},{64,72... | collective-permute-start | bytes 196616 | tf_op jit(solution)/shard_map/ppermute | solution.py:391

commit v4 on v3

--- a/solution.py
+++ b/solution.py
@@ -138,7 +138,8 @@
 
 
 def pick_kernel(nodes_hbm, send_hbm, rim_hbm, *refs):
-    hbm, (halo_hbm, outward, inward), state, refs = refs[:10], refs[10:13], refs[13:18], refs[18:]
+    hbm, (halo_hbm, early, outward, later) = refs[:10], refs[10:14]
+    state, refs = refs[14:19], refs[19:]
     nodes, send_index, rim_index, halo, in_sems, out_sems = refs[:6]
     into = [
         pltpu.make_async_copy(*pair, in_sems.at[i])
@@ -184,7 +185,9 @@
     into[2].wait()
     odd = odd_band()
     outward[...] = picked(hot(rim_index[pl.ds(1 - odd, 1), :]), own)
-    inward[...] = picked(hot(rim_index[pl.ds(odd, 1), :]), own)
+    inward = picked(hot(rim_index[pl.ds(odd, 1), :]), own)
+    early[...] = inward
+    later[...] = inward
 
     @pl.when(waits_long())
     def _():
@@ -204,8 +207,9 @@
 
 def finish_kernel(
     halo,
+    early,
     outward,
-    inward,
+    later,
     partial,
     columns,
     weights,
@@ -252,7 +256,7 @@
     from_out = pl.multiple_of(HALO_ROWS + RIM * odd, RIM)
     from_in = pl.multiple_of(HALO_ROWS + RIM - RIM * odd, RIM)
     table[pl.ds(from_out, RIM), :] = dot(outward[...], w_s).astype(BF16)
-    table[pl.ds(from_in, RIM), :] = dot(inward[...], w_s).astype(BF16)
+    table[pl.ds(from_in, RIM), :] = dot(early[...] + later[...], w_s).astype(BF16)
     w2 = weights[W_2 : W_2 + WIDTH, :]
     gain = vectors[GAIN : GAIN + 1, :]
     remote = table[...]
@@ -361,12 +365,13 @@
         pltpu.SemaphoreType.DMA((5,)),
         pltpu.SemaphoreType.DMA((LOCAL_TILES,)),
     ]
-    halo, outward, inward, *state = pl.pallas_call(
+    halo, early, outward, later, *state = pl.pallas_call(
         pick_kernel,
         in_specs=[hbm] * 13,
-        out_specs=[hbm] + [vmem] * 7,
+        out_specs=[hbm] + [vmem] * 8,
         out_shape=(
             pltpu.HBM((HALO_ROWS, WIDTH), BF16),
+            pltpu.VMEM((RIM, WIDTH), BF16),
             pltpu.VMEM((RIM, WIDTH), BF16),
             pltpu.VMEM((RIM, WIDTH), BF16),
         )
@@ -385,10 +390,11 @@
     )(nodes, in_hbm(send_index), in_hbm(rim_index), *far)
     halo = lax.all_to_all(halo, "lon", 0, 0, tiled=True)
     bands = lax.axis_size("lat")
+    early = lax.ppermute(early, "lat", [(i, i ^ 1) for i in range(bands) if i % SHELF <= 1])
     outward = lax.ppermute(
         outward, "lat", [(i, ((i + 1) ^ 1) - 1) for i in range(1, bands - 1)]
     )
-    inward = lax.ppermute(inward, "lat", [(i, i ^ 1) for i in range(bands)])
+    later = lax.ppermute(later, "lat", [(i, i ^ 1) for i in range(bands) if i % SHELF > 1])
     state = pl.pallas_call(
         local_kernel,
         in_specs=[hbm] * 10 + [vmem] * 5,
@@ -404,7 +410,7 @@
     )(*far, *map(in_vmem, state))
     return pl.pallas_call(
         finish_kernel,
-        in_specs=[vmem] * 8 + [pl.BlockSpec(memory_space=pltpu.SMEM)] + [hbm] * 4,
+        in_specs=[vmem] * 9 + [pl.BlockSpec(memory_space=pltpu.SMEM)] + [hbm] * 4,
         out_specs=[hbm, hbm],
         out_shape=(
             pltpu.HBM((NODE_ROWS, WIDTH), BF16),
@@ -423,7 +429,7 @@
         compiler_params=pltpu.CompilerParams(vmem_limit_bytes=24 * 1024 * 1024),
         name="edges_and_nodes",
     )(
-        *map(in_vmem, (halo, outward, inward, *state)),
+        *map(in_vmem, (halo, early, outward, later, *state)),
         edge_count,
         *map(in_hbm, (nodes, edges, node_w1, node_w2)),
     )

time: 34.1 us -> 33.4 us (0.979)
  the two profiles are of different devices: /device:TPU:15 before, /device:TPU:6 now
where the time goes in v4:
time: 33.4 us; the launch traced here: 32.7 us
  starting transfers between devices  18.5 us (55%)
  Pallas kernels  12.4 us (37%)
  between operations  1.33 us (4%)
  waiting for transfers between devices  0.45 us (1%)
    ppermute x1, starting transfers between devices, local(): lax.ppermute(outward, 'lat', [(i, (i + 1 ^ 1) - 1) for i in range(1, band...  8.84 us
    all_to_all x1, starting transfers between devices, local(): halo = lax.all_to_all(halo, 'lon', 0, 0, tiled=True)  7.11 us
    pallas_call x1, Pallas kernels, local(): pl.pallas_call(finish_kernel, in_specs=[vmem] * 9 + [pl.BlockSpec(memory_...  6.36 us
    pallas_call x1, Pallas kernels, local(): pl.pallas_call(pick_kernel, in_specs=[hbm] * 13, out_specs=[hbm] + [vmem]...  5.93 us
    ppermute x1, starting transfers between devices, local(): lax.ppermute(early, 'lat', [(i, i ^ 1) for i in range(bands) if i % SHELF...  1.91 us
  transfers between devices with their start and end apart: 4, of which 1 were waited for; matrix products, arithmetic and copies ran while one was open for 0% of the time, Pallas kernels for 0%

profile of v4, /device:TPU:6, one launch (start us, length us, event | category | flops | bytes accessed | tf_op | source)
XLA Modules:
  0.0 32.7 jit_solution(16890365105069810052)
XLA Ops:
  0.6 5.9 %pick_rows.1 = (bf16[512,256]{1,0:T(8,128)(2,1)}, bf16[128,256]{1,0:T(8,128)(2,1)S(1)}, bf16[128,256]{1,0:T(8,128)(2,1)S(1)}, bf16[128,256]{1,0:T(8,128)(2,1)S(1...) custom-call(bf16[256,256]{1,0:T(8,128)(2,1)} %nodes_hbm.3, ...), custom_call_target="tpu_custom_call" | custom-call | tf_op jit(solution)/shard_map/pick_rows/pallas_call | solution.py:368
  6.6 7.1 %all-to-all-start = ((bf16[8,64,256]{2,1,0:T(8,128)(2,1)}), bf16[8,64,256]{2,1,0:T(8,128)(2,1)S(1)}, u32[]{:S(2)}, u32[]{:S(2)}) async-start(bf16[8,64,256]{2,1,0:T(8,128)(2,1)} %bitcast.9), calls=%async_computation | async-start | bytes 524288 | tf_op jit(solution)/shard_map/all_to_all | solution.py:391
  13.7 1.9 %collective-permute-start = (bf16[128,256]{1,0:T(8,128)(2,1)S(1)}, bf16[128,256]{1,0:T(8,128)(2,1)S(1)}, u32[]{:S(2)}, u32[]{:S(2)}) collective-permute-start(bf16[128,256]{1,0:T(8,128)(2,1)S(1)} %get-tuple-element.17), channel_id=1, source_target_pairs={{0,8},{8,0},{192,200},{200,192},{384,392},{392,384},{576,584},{584... | collective-permute-start | bytes 196616 | tf_op jit(solution)/shard_map/ppermute | solution.py:393
  15.6 8.8 %collective-permute-start.1 = (bf16[128,256]{1,0:T(8,128)(2,1)S(1)}, bf16[128,256]{1,0:T(8,128)(2,1)S(1)}, u32[]{:S(2)}, u32[]{:S(2)}) collective-permute-start(bf16[128,256]{1,0:T(8,128)(2,1)S(1)} %get-tuple-element.18), channel_id=1, source_target_pairs={{8,16},{16,8},{24,32},{32,24},{40,48},{48,40},{56,64},{64,56},{72,... | collective-permute-start | bytes 196616 | tf_op jit(solution)/shard_map/ppermute | solution.py:394
  24.4 0.7 %collective-permute-start.2 = (bf16[128,256]{1,0:T(8,128)(2,1)S(1)}, bf16[128,256]{1,0:T(8,128)(2,1)S(1)}, u32[]{:S(2)}, u32[]{:S(2)}) collective-permute-start(bf16[128,256]{1,0:T(8,128)(2,1)S(1)} %get-tuple-element.19), channel_id=1, source_target_pairs={{16,24},{24,16},{32,40},{40,32},{48,56},{56,48},{64,72},{72,64},{8... | collective-permute-start | bytes 196616 | tf_op jit(solution)/shard_map/ppermute | solution.py:397
  25.8 0.2 local_edges.1
  25.9 0.0 collective-permute-done.early
  25.9 0.4 %collective-permute-done.1.outward = bf16[128,256]{1,0:T(8,128)(2,1)S(1)} collective-permute-done((bf16[128,256]{1,0:T(8,128)(2,1)S(1)}, bf16[128,256]{1,0:T(8,128)(2,1)S(1)}, u32[]{:S(2)}, u32[]{:S(2)}) %collective-permute-start.1) | collective-permute-done | bytes 65568 | tf_op jit(solution)/shard_map/ppermute | solution.py:394
  26.4 0.0 collective-permute-done.2.later
  26.4 0.0 all-to-all-done
  26.4 6.4 %edges_and_nodes.1 = (bf16[256,256]{1,0:T(8,128)(2,1)}, bf16[3072,256]{1,0:T(8,128)(2,1)}) custom-call(bf16[512,256]{1,0:T(8,128)(2,1)S(1)} %bitcast.8, bf16[128,256]{1,0:T(8,128)(2,1)S(1)} %collective-permute-done.early, bf16[128,256]{1,0:T(8,128)(2,1)S(1)} %collective-permute-done.1.outward, bf16[128,256]{1,0:T(8,128)(2,1)S(1)} %collective-permute-done.2.later, ...), custom_call_target="tpu_custom_call" | custom-call | tf_op jit(solution)/shard_map/edges_and_nodes/pallas_call | solution.py:411
Async XLA Ops:
  6.6 19.8 %all-to-all-start = ((bf16[8,64,256]{2,1,0:T(8,128)(2,1)}), bf16[8,64,256]{2,1,0:T(8,128)(2,1)S(1)}, u32[]{:S(2)}, u32[]{:S(2)}) async-start(bf16[8,64,256]{2,1,0:T(8,128)(2,1)} %bitcast.9), calls=%async_computation | async-start | bytes 524288 | tf_op jit(solution)/shard_map/all_to_all | solution.py:391
  13.7 12.3 %collective-permute-start = (bf16[128,256]{1,0:T(8,128)(2,1)S(1)}, bf16[128,256]{1,0:T(8,128)(2,1)S(1)}, u32[]{:S(2)}, u32[]{:S(2)}) collective-permute-start(bf16[128,256]{1,0:T(8,128)(2,1)S(1)} %get-tuple-element.17), channel_id=1, source_target_pairs={{0,8},{8,0},{192,200},{200,192},{384,392},{392,384},{576,584},{584... | collective-permute-start | bytes 196616 | tf_op jit(solution)/shard_map/ppermute | solution.py:393
  15.6 10.8 %collective-permute-start.1 = (bf16[128,256]{1,0:T(8,128)(2,1)S(1)}, bf16[128,256]{1,0:T(8,128)(2,1)S(1)}, u32[]{:S(2)}, u32[]{:S(2)}) collective-permute-start(bf16[128,256]{1,0:T(8,128)(2,1)S(1)} %get-tuple-element.18), channel_id=1, source_target_pairs={{8,16},{16,8},{24,32},{32,24},{40,48},{48,40},{56,64},{64,56},{72,... | collective-permute-start | bytes 196616 | tf_op jit(solution)/shard_map/ppermute | solution.py:394
  24.4 1.9 %collective-permute-start.2 = (bf16[128,256]{1,0:T(8,128)(2,1)S(1)}, bf16[128,256]{1,0:T(8,128)(2,1)S(1)}, u32[]{:S(2)}, u32[]{:S(2)}) collective-permute-start(bf16[128,256]{1,0:T(8,128)(2,1)S(1)} %get-tuple-element.19), channel_id=1, source_target_pairs={{16,24},{24,16},{32,40},{40,32},{48,56},{56,48},{64,72},{72,64},{8... | collective-permute-start | bytes 196616 | tf_op jit(solution)/shard_map/ppermute | solution.py:397

commit v5 on v4

--- a/solution.py
+++ b/solution.py
@@ -262,7 +262,7 @@
     remote = table[...]
     lane = lax.broadcasted_iota(I16, (TILE, LANES), 1)
     one, zero = jnp.ones((), BF16), jnp.zeros((), BF16)
-    node = lax.broadcasted_iota(I32, (NODE_ROWS, LANES), 0)
+    node = lax.broadcasted_iota(I16, (NODE_ROWS, LANES), 0)
     messages = jnp.zeros((NODE_ROWS, WIDTH), F32)
     count = count_smem[0]
 
@@ -276,11 +276,13 @@
         spot = lax.broadcasted_iota(I32, (TILE, 1), 0) + t * TILE
         update = scaled(dot(silu(pre).astype(BF16), w2), gain, spot < count).astype(BF16)
         loads[t].wait()
-        edges[rows, :] = (edges[rows, :].astype(F32) + update.astype(F32)).astype(BF16)
+        edges[rows, :] = edges[rows, :] + update
         stores[t].start()
         member = jnp.concatenate(
             [
-                jnp.where(node == receivers[g : g + 1, :], 1.0, 0.0).astype(BF16)
+                jnp.where(
+                    node == jnp.broadcast_to(receivers[g : g + 1, :], node.shape).astype(I16), one, zero
+                )
                 for g in range(t * TILE // LANES, (t + 1) * TILE // LANES)
             ],
             axis=1,

time: 33.4 us -> 32.9 us (0.985)
  Pallas kernels: 12.4 us -> 11.9 us
    pallas_call x1, Pallas kernels: 6.36 us -> 5.85 us  [local(): pl.pallas_call(finish_kernel, in_specs=[vmem] * 9 + [pl.BlockSpec(memory_...]
where the time goes in v5:
time: 32.9 us; the launch traced here: 32.2 us
  starting transfers between devices  18.5 us (56%)
  Pallas kernels  11.9 us (36%)
  between operations  1.33 us (4%)
  waiting for transfers between devices  0.45 us (1%)
    ppermute x1, starting transfers between devices, local(): lax.ppermute(outward, 'lat', [(i, (i + 1 ^ 1) - 1) for i in range(1, band...  8.84 us
    all_to_all x1, starting transfers between devices, local(): halo = lax.all_to_all(halo, 'lon', 0, 0, tiled=True)  7.11 us
    pallas_call x1, Pallas kernels, local(): pl.pallas_call(pick_kernel, in_specs=[hbm] * 13, out_specs=[hbm] + [vmem]...  5.93 us
    pallas_call x1, Pallas kernels, local(): pl.pallas_call(finish_kernel, in_specs=[vmem] * 9 + [pl.BlockSpec(memory_...  5.85 us
    ppermute x1, starting transfers between devices, local(): lax.ppermute(early, 'lat', [(i, i ^ 1) for i in range(bands) if i % SHELF...  1.91 us
    ppermute x1, starting transfers between devices, local(): lax.ppermute(later, 'lat', [(i, i ^ 1) for i in range(bands) if i % SHELF...  0.66 us
  transfers between devices with their start and end apart: 4, of which 1 were waited for; matrix products, arithmetic and copies ran while one was open for 0% of the time, Pallas kernels for 0%

profile of v5, /device:TPU:6, one launch (start us, length us, event | category | flops | bytes accessed | tf_op | source)
XLA Modules:
  0.0 32.2 jit_solution(8921080543919987714)
XLA Ops:
  0.6 5.9 %pick_rows.1 = (bf16[512,256]{1,0:T(8,128)(2,1)}, bf16[128,256]{1,0:T(8,128)(2,1)S(1)}, bf16[128,256]{1,0:T(8,128)(2,1)S(1)}, bf16[128,256]{1,0:T(8,128)(2,1)S(1...) custom-call(bf16[256,256]{1,0:T(8,128)(2,1)} %nodes_hbm.3, ...), custom_call_target="tpu_custom_call" | custom-call | tf_op jit(solution)/shard_map/pick_rows/pallas_call | solution.py:370
  6.6 7.1 %all-to-all-start = ((bf16[8,64,256]{2,1,0:T(8,128)(2,1)}), bf16[8,64,256]{2,1,0:T(8,128)(2,1)S(1)}, u32[]{:S(2)}, u32[]{:S(2)}) async-start(bf16[8,64,256]{2,1,0:T(8,128)(2,1)} %bitcast.9), calls=%async_computation | async-start | bytes 524288 | tf_op jit(solution)/shard_map/all_to_all | solution.py:393
  13.7 1.9 %collective-permute-start = (bf16[128,256]{1,0:T(8,128)(2,1)S(1)}, bf16[128,256]{1,0:T(8,128)(2,1)S(1)}, u32[]{:S(2)}, u32[]{:S(2)}) collective-permute-start(bf16[128,256]{1,0:T(8,128)(2,1)S(1)} %get-tuple-element.17), channel_id=1, source_target_pairs={{0,8},{8,0},{192,200},{200,192},{384,392},{392,384},{576,584},{584... | collective-permute-start | bytes 196616 | tf_op jit(solution)/shard_map/ppermute | solution.py:395
  15.6 8.8 %collective-permute-start.1 = (bf16[128,256]{1,0:T(8,128)(2,1)S(1)}, bf16[128,256]{1,0:T(8,128)(2,1)S(1)}, u32[]{:S(2)}, u32[]{:S(2)}) collective-permute-start(bf16[128,256]{1,0:T(8,128)(2,1)S(1)} %get-tuple-element.18), channel_id=1, source_target_pairs={{8,16},{16,8},{24,32},{32,24},{40,48},{48,40},{56,64},{64,56},{72,... | collective-permute-start | bytes 196616 | tf_op jit(solution)/shard_map/ppermute | solution.py:396
  24.4 0.7 %collective-permute-start.2 = (bf16[128,256]{1,0:T(8,128)(2,1)S(1)}, bf16[128,256]{1,0:T(8,128)(2,1)S(1)}, u32[]{:S(2)}, u32[]{:S(2)}) collective-permute-start(bf16[128,256]{1,0:T(8,128)(2,1)S(1)} %get-tuple-element.19), channel_id=1, source_target_pairs={{16,24},{24,16},{32,40},{40,32},{48,56},{56,48},{64,72},{72,64},{8... | collective-permute-start | bytes 196616 | tf_op jit(solution)/shard_map/ppermute | solution.py:399
  25.8 0.2 local_edges.1
  25.9 0.0 collective-permute-done.early
  25.9 0.4 %collective-permute-done.1.outward = bf16[128,256]{1,0:T(8,128)(2,1)S(1)} collective-permute-done((bf16[128,256]{1,0:T(8,128)(2,1)S(1)}, bf16[128,256]{1,0:T(8,128)(2,1)S(1)}, u32[]{:S(2)}, u32[]{:S(2)}) %collective-permute-start.1) | collective-permute-done | bytes 65568 | tf_op jit(solution)/shard_map/ppermute | solution.py:396
  26.4 0.0 collective-permute-done.2.later
  26.4 0.0 all-to-all-done
  26.4 5.9 %edges_and_nodes.1 = (bf16[256,256]{1,0:T(8,128)(2,1)}, bf16[3072,256]{1,0:T(8,128)(2,1)}) custom-call(bf16[512,256]{1,0:T(8,128)(2,1)S(1)} %bitcast.8, bf16[128,256]{1,0:T(8,128)(2,1)S(1)} %collective-permute-done.early, bf16[128,256]{1,0:T(8,128)(2,1)S(1)} %collective-permute-done.1.outward, bf16[128,256]{1,0:T(8,128)(2,1)S(1)} %collective-permute-done.2.later, ...), custom_call_target="tpu_custom_call" | custom-call | tf_op jit(solution)/shard_map/edges_and_nodes/pallas_call | solution.py:413
Async XLA Ops:
  6.6 19.8 %all-to-all-start = ((bf16[8,64,256]{2,1,0:T(8,128)(2,1)}), bf16[8,64,256]{2,1,0:T(8,128)(2,1)S(1)}, u32[]{:S(2)}, u32[]{:S(2)}) async-start(bf16[8,64,256]{2,1,0:T(8,128)(2,1)} %bitcast.9), calls=%async_computation | async-start | bytes 524288 | tf_op jit(solution)/shard_map/all_to_all | solution.py:393
  13.7 12.3 %collective-permute-start = (bf16[128,256]{1,0:T(8,128)(2,1)S(1)}, bf16[128,256]{1,0:T(8,128)(2,1)S(1)}, u32[]{:S(2)}, u32[]{:S(2)}) collective-permute-start(bf16[128,256]{1,0:T(8,128)(2,1)S(1)} %get-tuple-element.17), channel_id=1, source_target_pairs={{0,8},{8,0},{192,200},{200,192},{384,392},{392,384},{576,584},{584... | collective-permute-start | bytes 196616 | tf_op jit(solution)/shard_map/ppermute | solution.py:395
  15.6 10.8 %collective-permute-start.1 = (bf16[128,256]{1,0:T(8,128)(2,1)S(1)}, bf16[128,256]{1,0:T(8,128)(2,1)S(1)}, u32[]{:S(2)}, u32[]{:S(2)}) collective-permute-start(bf16[128,256]{1,0:T(8,128)(2,1)S(1)} %get-tuple-element.18), channel_id=1, source_target_pairs={{8,16},{16,8},{24,32},{32,24},{40,48},{48,40},{56,64},{64,56},{72,... | collective-permute-start | bytes 196616 | tf_op jit(solution)/shard_map/ppermute | solution.py:396
  24.4 1.9 %collective-permute-start.2 = (bf16[128,256]{1,0:T(8,128)(2,1)S(1)}, bf16[128,256]{1,0:T(8,128)(2,1)S(1)}, u32[]{:S(2)}, u32[]{:S(2)}) collective-permute-start(bf16[128,256]{1,0:T(8,128)(2,1)S(1)} %get-tuple-element.19), channel_id=1, source_target_pairs={{16,24},{24,16},{32,40},{40,32},{48,56},{56,48},{64,72},{72,64},{8... | collective-permute-start | bytes 196616 | tf_op jit(solution)/shard_map/ppermute | solution.py:399

commit v6 on v5

--- a/solution.py
+++ b/solution.py
@@ -275,7 +275,9 @@
         pre = partial[rows, :].astype(F32) + dot(chosen, remote)
         spot = lax.broadcasted_iota(I32, (TILE, 1), 0) + t * TILE
         update = scaled(dot(silu(pre).astype(BF16), w2), gain, spot < count).astype(BF16)
-        loads[t].wait()
+        if t == 0:
+            for copy in loads:
+                copy.wait()
         edges[rows, :] = edges[rows, :] + update
         stores[t].start()
         member = jnp.concatenate(

time: 32.9 us -> 32.7 us (level)
  the two profiles are of different devices: /device:TPU:6 before, /device:TPU:73 now
where the time goes in v6:
time: 32.7 us; the launch traced here: 32.4 us
  starting transfers between devices  18.9 us (58%)
  Pallas kernels  12.1 us (37%)
  between operations  1.35 us (4%)
    all_to_all x1, starting transfers between devices, local(): halo = lax.all_to_all(halo, 'lon', 0, 0, tiled=True)  7 us
    ppermute x1, starting transfers between devices, local(): lax.ppermute(later, 'lat', [(i, i ^ 1) for i in range(bands) if i % SHELF...  6.17 us
    pallas_call x1, Pallas kernels, local(): pl.pallas_call(finish_kernel, in_specs=[vmem] * 9 + [pl.BlockSpec(memory_...  5.67 us
    ppermute x1, starting transfers between devices, local(): lax.ppermute(outward, 'lat', [(i, (i + 1 ^ 1) - 1) for i in range(1, band...  5.12 us
    pallas_call x1, Pallas kernels, local(): pl.pallas_call(local_kernel, in_specs=[hbm] * 10 + [vmem] * 5, out_specs=...  4.4 us
    pallas_call x1, Pallas kernels, local(): pl.pallas_call(pick_kernel, in_specs=[hbm] * 13, out_specs=[hbm] + [vmem]...  2.01 us
  transfers between devices with their start and end apart: 4, of which 0 were waited for; matrix products, arithmetic and copies ran while one was open for 0% of the time, Pallas kernels for 14%

profile of v6, /device:TPU:73, one launch (start us, length us, event | category | flops | bytes accessed | tf_op | source)
XLA Modules:
  0.0 32.4 jit_solution(120752697782300587)
XLA Ops:
  0.6 2.0 %pick_rows.1 = (bf16[512,256]{1,0:T(8,128)(2,1)}, bf16[128,256]{1,0:T(8,128)(2,1)S(1)}, bf16[128,256]{1,0:T(8,128)(2,1)S(1)}, bf16[128,256]{1,0:T(8,128)(2,1)S(1...) custom-call(bf16[256,256]{1,0:T(8,128)(2,1)} %nodes_hbm.3, ...), custom_call_target="tpu_custom_call" | custom-call | tf_op jit(solution)/shard_map/pick_rows/pallas_call | solution.py:372
  2.6 7.0 %all-to-all-start = ((bf16[8,64,256]{2,1,0:T(8,128)(2,1)}), bf16[8,64,256]{2,1,0:T(8,128)(2,1)S(1)}, u32[]{:S(2)}, u32[]{:S(2)}) async-start(bf16[8,64,256]{2,1,0:T(8,128)(2,1)} %bitcast.9), calls=%async_computation | async-start | bytes 524288 | tf_op jit(solution)/shard_map/all_to_all | solution.py:395
  9.6 0.7 %collective-permute-start = (bf16[128,256]{1,0:T(8,128)(2,1)S(1)}, bf16[128,256]{1,0:T(8,128)(2,1)S(1)}, u32[]{:S(2)}, u32[]{:S(2)}) collective-permute-start(bf16[128,256]{1,0:T(8,128)(2,1)S(1)} %get-tuple-element.17), channel_id=1, source_target_pairs={{0,8},{8,0},{192,200},{200,192},{384,392},{392,384},{576,584},{584... | collective-permute-start | bytes 196616 | tf_op jit(solution)/shard_map/ppermute | solution.py:397
  10.3 5.1 %collective-permute-start.1 = (bf16[128,256]{1,0:T(8,128)(2,1)S(1)}, bf16[128,256]{1,0:T(8,128)(2,1)S(1)}, u32[]{:S(2)}, u32[]{:S(2)}) collective-permute-start(bf16[128,256]{1,0:T(8,128)(2,1)S(1)} %get-tuple-element.18), channel_id=1, source_target_pairs={{8,16},{16,8},{24,32},{32,24},{40,48},{48,40},{56,64},{64,56},{72,... | collective-permute-start | bytes 196616 | tf_op jit(solution)/shard_map/ppermute | solution.py:398
  15.4 6.2 %collective-permute-start.2 = (bf16[128,256]{1,0:T(8,128)(2,1)S(1)}, bf16[128,256]{1,0:T(8,128)(2,1)S(1)}, u32[]{:S(2)}, u32[]{:S(2)}) collective-permute-start(bf16[128,256]{1,0:T(8,128)(2,1)S(1)} %get-tuple-element.19), channel_id=1, source_target_pairs={{16,24},{24,16},{32,40},{40,32},{48,56},{56,48},{64,72},{72,64},{8... | collective-permute-start | bytes 196616 | tf_op jit(solution)/shard_map/ppermute | solution.py:401
  22.3 4.4 %local_edges.1 = (bf16[3072,256]{1,0:T(8,128)(2,1)S(1)}, s16[3072,128]{1,0:T(8,128)(2,1)S(1)}, bf16[512,256]{1,0:T(8,128)(2,1)S(1)}, f32[8,256]{1,0:T(8,128)S(1)}, s32[24,128]{1,0:T(8,128)S(1)}) custom-call(bf16[256,256]{1,0:T(8,128)(2,1)} %nodes_hbm.3, ...), custom_call_target="tpu_custom_call", output_to_operand_aliasing={{0}: (10, {}), {1}: (11, {}), {2}: (12, {}), {3}: (13, {}),... | custom-call | flops 1207959552 | bytes 8000000 | tf_op jit(solution)/shard_map/local_edges/pallas_call | solution.py:402
  26.7 0.0 collective-permute-done.early
  26.7 0.0 collective-permute-done.1.outward
  26.7 0.0 collective-permute-done.2.later
  26.7 0.0 all-to-all-done
  26.7 5.7 %edges_and_nodes.1 = (bf16[256,256]{1,0:T(8,128)(2,1)}, bf16[3072,256]{1,0:T(8,128)(2,1)}) custom-call(bf16[512,256]{1,0:T(8,128)(2,1)S(1)} %bitcast.8, bf16[128,256]{1,0:T(8,128)(2,1)S(1)} %collective-permute-done.early, bf16[128,256]{1,0:T(8,128)(2,1)S(1)} %collective-permute-done.1.outward, bf16[128,256]{1,0:T(8,128)(2,1)S(1)} %collective-permute-done.2.later, ...), custom_call_target="tpu_custom_call" | custom-call | tf_op jit(solution)/shard_map/edges_and_nodes/pallas_call | solution.py:415
Async XLA Ops:
  2.6 24.1 %all-to-all-start = ((bf16[8,64,256]{2,1,0:T(8,128)(2,1)}), bf16[8,64,256]{2,1,0:T(8,128)(2,1)S(1)}, u32[]{:S(2)}, u32[]{:S(2)}) async-start(bf16[8,64,256]{2,1,0:T(8,128)(2,1)} %bitcast.9), calls=%async_computation | async-start | bytes 524288 | tf_op jit(solution)/shard_map/all_to_all | solution.py:395
  9.6 17.0 %collective-permute-start = (bf16[128,256]{1,0:T(8,128)(2,1)S(1)}, bf16[128,256]{1,0:T(8,128)(2,1)S(1)}, u32[]{:S(2)}, u32[]{:S(2)}) collective-permute-start(bf16[128,256]{1,0:T(8,128)(2,1)S(1)} %get-tuple-element.17), channel_id=1, source_target_pairs={{0,8},{8,0},{192,200},{200,192},{384,392},{392,384},{576,584},{584... | collective-permute-start | bytes 196616 | tf_op jit(solution)/shard_map/ppermute | solution.py:397
  10.3 16.4 %collective-permute-start.1 = (bf16[128,256]{1,0:T(8,128)(2,1)S(1)}, bf16[128,256]{1,0:T(8,128)(2,1)S(1)}, u32[]{:S(2)}, u32[]{:S(2)}) collective-permute-start(bf16[128,256]{1,0:T(8,128)(2,1)S(1)} %get-tuple-element.18), channel_id=1, source_target_pairs={{8,16},{16,8},{24,32},{32,24},{40,48},{48,40},{56,64},{64,56},{72,... | collective-permute-start | bytes 196616 | tf_op jit(solution)/shard_map/ppermute | solution.py:398
  15.4 11.3 %collective-permute-start.2 = (bf16[128,256]{1,0:T(8,128)(2,1)S(1)}, bf16[128,256]{1,0:T(8,128)(2,1)S(1)}, u32[]{:S(2)}, u32[]{:S(2)}) collective-permute-start(bf16[128,256]{1,0:T(8,128)(2,1)S(1)} %get-tuple-element.19), channel_id=1, source_target_pairs={{16,24},{24,16},{32,40},{40,32},{48,56},{56,48},{64,72},{72,64},{8... | collective-permute-start | bytes 196616 | tf_op jit(solution)/shard_map/ppermute | solution.py:401

commit v7 on v6

--- a/solution.py
+++ b/solution.py
@@ -52,7 +52,7 @@
 
 def waits_long():
     lat, lon = lax.axis_index("lat"), lax.axis_index("lon")
-    return (lat + lon > 0) & (lax.rem(lat, SHELF) <= 1)
+    return (lat + lon > 0) & (lax.rem(lat, SHELF) <= 3)
 
 
 def odd_band():

time: 32.7 us -> 32.6 us (level)
  the two profiles are of different devices: /device:TPU:73 before, /device:TPU:6 now
where the time goes in v7:
time: 32.6 us; the launch traced here: 32.1 us
  starting transfers between devices  18.5 us (57%)
  Pallas kernels  11.7 us (36%)
  between operations  1.33 us (4%)
  waiting for transfers between devices  0.45 us (1%)
    ppermute x1, starting transfers between devices, local(): lax.ppermute(outward, 'lat', [(i, (i + 1 ^ 1) - 1) for i in range(1, band...  8.84 us
    all_to_all x1, starting transfers between devices, local(): halo = lax.all_to_all(halo, 'lon', 0, 0, tiled=True)  7.11 us
    pallas_call x1, Pallas kernels, local(): pl.pallas_call(pick_kernel, in_specs=[hbm] * 13, out_specs=[hbm] + [vmem]...  5.93 us
    pallas_call x1, Pallas kernels, local(): pl.pallas_call(finish_kernel, in_specs=[vmem] * 9 + [pl.BlockSpec(memory_...  5.67 us
    ppermute x1, starting transfers between devices, local(): lax.ppermute(early, 'lat', [(i, i ^ 1) for i in range(bands) if i % SHELF...  1.91 us
    ppermute x1, starting transfers between devices, local(): lax.ppermute(later, 'lat', [(i, i ^ 1) for i in range(bands) if i % SHELF...  0.66 us
  transfers between devices with their start and end apart: 4, of which 1 were waited for; matrix products, arithmetic and copies ran while one was open for 0% of the time, Pallas kernels for 0%

profile of v7, /device:TPU:6, one launch (start us, length us, event | category | flops | bytes accessed | tf_op | source)
XLA Modules:
  0.0 32.1 jit_solution(12105048917872202506)
XLA Ops:
  0.6 5.9 %pick_rows.1 = (bf16[512,256]{1,0:T(8,128)(2,1)}, bf16[128,256]{1,0:T(8,128)(2,1)S(1)}, bf16[128,256]{1,0:T(8,128)(2,1)S(1)}, bf16[128,256]{1,0:T(8,128)(2,1)S(1...) custom-call(bf16[256,256]{1,0:T(8,128)(2,1)} %nodes_hbm.3, ...), custom_call_target="tpu_custom_call" | custom-call | tf_op jit(solution)/shard_map/pick_rows/pallas_call | solution.py:372
  6.6 7.1 %all-to-all-start = ((bf16[8,64,256]{2,1,0:T(8,128)(2,1)}), bf16[8,64,256]{2,1,0:T(8,128)(2,1)S(1)}, u32[]{:S(2)}, u32[]{:S(2)}) async-start(bf16[8,64,256]{2,1,0:T(8,128)(2,1)} %bitcast.9), calls=%async_computation | async-start | bytes 524288 | tf_op jit(solution)/shard_map/all_to_all | solution.py:395
  13.7 1.9 %collective-permute-start = (bf16[128,256]{1,0:T(8,128)(2,1)S(1)}, bf16[128,256]{1,0:T(8,128)(2,1)S(1)}, u32[]{:S(2)}, u32[]{:S(2)}) collective-permute-start(bf16[128,256]{1,0:T(8,128)(2,1)S(1)} %get-tuple-element.17), channel_id=1, source_target_pairs={{0,8},{8,0},{192,200},{200,192},{384,392},{392,384},{576,584},{584... | collective-permute-start | bytes 196616 | tf_op jit(solution)/shard_map/ppermute | solution.py:397
  15.6 8.8 %collective-permute-start.1 = (bf16[128,256]{1,0:T(8,128)(2,1)S(1)}, bf16[128,256]{1,0:T(8,128)(2,1)S(1)}, u32[]{:S(2)}, u32[]{:S(2)}) collective-permute-start(bf16[128,256]{1,0:T(8,128)(2,1)S(1)} %get-tuple-element.18), channel_id=1, source_target_pairs={{8,16},{16,8},{24,32},{32,24},{40,48},{48,40},{56,64},{64,56},{72,... | collective-permute-start | bytes 196616 | tf_op jit(solution)/shard_map/ppermute | solution.py:398
  24.4 0.7 %collective-permute-start.2 = (bf16[128,256]{1,0:T(8,128)(2,1)S(1)}, bf16[128,256]{1,0:T(8,128)(2,1)S(1)}, u32[]{:S(2)}, u32[]{:S(2)}) collective-permute-start(bf16[128,256]{1,0:T(8,128)(2,1)S(1)} %get-tuple-element.19), channel_id=1, source_target_pairs={{16,24},{24,16},{32,40},{40,32},{48,56},{56,48},{64,72},{72,64},{8... | collective-permute-start | bytes 196616 | tf_op jit(solution)/shard_map/ppermute | solution.py:401
  25.8 0.2 local_edges.1
  25.9 0.0 collective-permute-done.early
  25.9 0.4 %collective-permute-done.1.outward = bf16[128,256]{1,0:T(8,128)(2,1)S(1)} collective-permute-done((bf16[128,256]{1,0:T(8,128)(2,1)S(1)}, bf16[128,256]{1,0:T(8,128)(2,1)S(1)}, u32[]{:S(2)}, u32[]{:S(2)}) %collective-permute-start.1) | collective-permute-done | bytes 65568 | tf_op jit(solution)/shard_map/ppermute | solution.py:398
  26.4 0.0 collective-permute-done.2.later
  26.4 0.0 all-to-all-done
  26.4 5.7 %edges_and_nodes.1 = (bf16[256,256]{1,0:T(8,128)(2,1)}, bf16[3072,256]{1,0:T(8,128)(2,1)}) custom-call(bf16[512,256]{1,0:T(8,128)(2,1)S(1)} %bitcast.8, bf16[128,256]{1,0:T(8,128)(2,1)S(1)} %collective-permute-done.early, bf16[128,256]{1,0:T(8,128)(2,1)S(1)} %collective-permute-done.1.outward, bf16[128,256]{1,0:T(8,128)(2,1)S(1)} %collective-permute-done.2.later, ...), custom_call_target="tpu_custom_call" | custom-call | tf_op jit(solution)/shard_map/edges_and_nodes/pallas_call | solution.py:415
Async XLA Ops:
  6.6 19.8 %all-to-all-start = ((bf16[8,64,256]{2,1,0:T(8,128)(2,1)}), bf16[8,64,256]{2,1,0:T(8,128)(2,1)S(1)}, u32[]{:S(2)}, u32[]{:S(2)}) async-start(bf16[8,64,256]{2,1,0:T(8,128)(2,1)} %bitcast.9), calls=%async_computation | async-start | bytes 524288 | tf_op jit(solution)/shard_map/all_to_all | solution.py:395
  13.7 12.3 %collective-permute-start = (bf16[128,256]{1,0:T(8,128)(2,1)S(1)}, bf16[128,256]{1,0:T(8,128)(2,1)S(1)}, u32[]{:S(2)}, u32[]{:S(2)}) collective-permute-start(bf16[128,256]{1,0:T(8,128)(2,1)S(1)} %get-tuple-element.17), channel_id=1, source_target_pairs={{0,8},{8,0},{192,200},{200,192},{384,392},{392,384},{576,584},{584... | collective-permute-start | bytes 196616 | tf_op jit(solution)/shard_map/ppermute | solution.py:397
  15.6 10.8 %collective-permute-start.1 = (bf16[128,256]{1,0:T(8,128)(2,1)S(1)}, bf16[128,256]{1,0:T(8,128)(2,1)S(1)}, u32[]{:S(2)}, u32[]{:S(2)}) collective-permute-start(bf16[128,256]{1,0:T(8,128)(2,1)S(1)} %get-tuple-element.18), channel_id=1, source_target_pairs={{8,16},{16,8},{24,32},{32,24},{40,48},{48,40},{56,64},{64,56},{72,... | collective-permute-start | bytes 196616 | tf_op jit(solution)/shard_map/ppermute | solution.py:398
  24.4 1.9 %collective-permute-start.2 = (bf16[128,256]{1,0:T(8,128)(2,1)S(1)}, bf16[128,256]{1,0:T(8,128)(2,1)S(1)}, u32[]{:S(2)}, u32[]{:S(2)}) collective-permute-start(bf16[128,256]{1,0:T(8,128)(2,1)S(1)} %get-tuple-element.19), channel_id=1, source_target_pairs={{16,24},{24,16},{32,40},{40,32},{48,56},{56,48},{64,72},{72,64},{8... | collective-permute-start | bytes 196616 | tf_op jit(solution)/shard_map/ppermute | solution.py:401
